TPU v7x, 128 devices: a whole 4x4x4 slice. The times are simulated.
128 devices in a mesh: tm: 2 (over x_hi), chan: 64 (over y, x_lo, z, core).
Axes of the slice: x: 4 (x_hi: 2, x_lo: 2; x = x_hi * 2 + x_lo), y: 4, z: 4, core: 2. Of those that a mesh axis runs over, the one named last changes fastest.
Arguments:
- strain: bfloat16 [6, 16000, 4096], P('tm', 'chan'), may hold values from -6 to 6
- live_mask: int32 [4096], P('chan'), may hold values 0 or 1
- block_pairs: int32 [2, 64, 2], P(None, 'chan'), may hold values from 0 to 63, as said below
Outputs:
- correlations: bfloat16 [2, 64, 64, 64, 1024], P('tm', 'chan')
Inputs may be any that keep to these rules, and one draw needn't show every extreme that they name: `block_pairs`: each row holds two channel-block numbers, the first not above the second; every block number appears in some row.
All inputs are finite; a program needn't handle non-finite values. No bound on the sum of `live_mask` on one device may be relied on, other than what follows from the above.
Results may differ from a plain program's by a relative error of at most 0.01.
Values may be sent and summed in bfloat16 or wider, within the bound.
No kernel may reach another device: no remote copies, remote signals or barrier semaphores. Data moves between devices by JAX's collectives and lax.ppermute only.
A program may use at most 128 MiB of HBM per device.

v0:
```python
import math

import jax
import jax.numpy as jnp
from jax import lax
from jax.sharding import PartitionSpec as P

CB = 64
W = 16000
WIN_DEV = 3
K0 = 64
F = 256
HALF = 32
LAGS = 1024


whiten_eps = 1e-05


def forward_table():
    samples = jnp.arange(W, dtype=jnp.int32)[:, None]
    bins = (K0 - HALF + jnp.arange(F + 2 * HALF, dtype=jnp.int32))[None, :]
    phase_index = samples * bins % W
    angles = 2.0 * math.pi / W * phase_index.astype(jnp.float32)
    window_shape = (
        0.5
        - 0.5
        * jnp.cos(2.0 * math.pi / W * jnp.arange(W, dtype=jnp.int32).astype(jnp.float32))[:, None]
    )
    return jnp.concatenate(
        [jnp.cos(angles) * window_shape, -jnp.sin(angles) * window_shape], 1
    ).astype(jnp.bfloat16)


def backward_table():
    freqs = (K0 + jnp.arange(F, dtype=jnp.int32))[:, None]
    lag_steps = (jnp.arange(LAGS, dtype=jnp.int32) - LAGS // 2)[None, :]
    phase_index = freqs * lag_steps % W
    angles = 2.0 * math.pi / W * phase_index.astype(jnp.float32)
    factor = 1.0 / math.sqrt(WIN_DEV * F)
    return jnp.concatenate([jnp.cos(angles) * factor, -jnp.sin(angles) * factor], 0).astype(
        jnp.bfloat16
    )


def smoothing_matrix():
    rows = jnp.arange(F + 2 * HALF, dtype=jnp.int32)[:, None]
    cols = jnp.arange(F, dtype=jnp.int32)[None, :]
    inside = jnp.abs(rows - cols - HALF) <= HALF
    return jnp.where(inside, 1.0 / (2 * HALF + 1), 0.0).astype(jnp.float32)


def band_weights():
    freqs = jnp.arange(F, dtype=jnp.int32).astype(jnp.float32) + 0.5
    edge_ramp = jnp.minimum(freqs, F - freqs) / (F / 4.0)
    return jnp.where(edge_ramp < 1.0, 0.5 - 0.5 * jnp.cos(math.pi * edge_ramp), 1.0)


def cross_spectrum(left_block, right_block):
    left_real, left_imag = (left_block[..., :F], left_block[..., F:])
    right_real, right_imag = (right_block[..., :F], right_block[..., F:])
    real_sum = jnp.einsum(
        "wif,wjf->ijf", left_real, right_real, preferred_element_type=jnp.float32
    ) + jnp.einsum("wif,wjf->ijf", left_imag, right_imag, preferred_element_type=jnp.float32)
    imag_sum = jnp.einsum(
        "wif,wjf->ijf", left_imag, right_real, preferred_element_type=jnp.float32
    ) - jnp.einsum("wif,wjf->ijf", left_real, right_imag, preferred_element_type=jnp.float32)
    return jnp.concatenate([real_sum, imag_sum], -1).reshape(CB * CB, 2 * F).astype(jnp.bfloat16)


def per_device(strain, live_mask, block_pairs):
    forward = forward_table()
    smoother = smoothing_matrix()
    band_taper = band_weights()
    backward = backward_table()
    live_rows = live_mask.astype(jnp.float32)
    width = F + 2 * HALF
    groups = lax.axis_size("tm")
    pairs_here = block_pairs.shape[1]
    raw_spec = jnp.einsum(
        "wnc,nk->wck",
        lax.all_to_all(strain, "chan", split_axis=2, concat_axis=1, tiled=True),
        forward,
        preferred_element_type=jnp.float32,
    )
    real_part = raw_spec[..., :width]
    imag_part = raw_spec[..., width:]
    magnitude = jnp.sqrt(real_part * real_part + imag_part * imag_part)
    smooth = jnp.dot(magnitude, smoother, precision=lax.Precision.HIGHEST)
    weighting = band_taper[None, None, :] * live_rows[None, :, None] / (smooth + whiten_eps)
    spectra = jnp.concatenate(
        [real_part[..., HALF : HALF + F] * weighting, imag_part[..., HALF : HALF + F] * weighting],
        -1,
    ).astype(jnp.bfloat16)
    win_count = spectra.shape[0]
    everyone = lax.all_gather(spectra, "chan", axis=1, tiled=True)

    def take_block(block_index):
        return lax.dynamic_slice_in_dim(everyone, block_index * CB, CB, 1)

    picked = lax.map(take_block, block_pairs.reshape(-1))
    picked = picked.reshape(groups, pairs_here, 2, win_count, CB, 2 * F)
    chosen = picked.reshape(-1, 2, win_count, CB, 2 * F)

    def pair_lags(pair_blocks):
        return jnp.dot(
            cross_spectrum(pair_blocks[0], pair_blocks[1]),
            backward,
            preferred_element_type=jnp.float32,
        )

    lagged = lax.map(pair_lags, chosen)
    return lax.psum_scatter(
        lagged.reshape(1 * lax.axis_size("tm"), pairs_here, CB, CB, LAGS).astype(jnp.bfloat16),
        "tm",
        scatter_dimension=0,
        tiled=True,
    )


def solution(mesh):
    in_specs = (P("tm", "chan", None), P("chan"), P(None, "chan", None))
    out_specs = P("tm", "chan", None, None, None)
    return jax.shard_map(
        per_device, mesh=mesh, in_specs=in_specs, out_specs=out_specs, check_vma=False
    )
```

profile of v0, /device:TPU:1, one launch (start us, length us, event | category | flops | bytes accessed | tf_op | source)
XLA Modules:
  0.0 590.3 jit_solution(14845604365244525691)
XLA Ops:
  6.5 13.0 %copy.11 = bf16[3,250,4096]{1,0,2:T(4,128)(2,1)} copy(bf16[3,250,4096]{2,1,0:T(8,128)(2,1)} %param.7) | data formatting | bytes 12288000 | tf_op args[0]
  19.6 11.3 %all-to-all-start = ((bf16[3,250,4096]{1,0,2:T(4,128)(2,1)}), bf16[3,250,4096]{1,0,2:T(4,128)(2,1)}, u32[]{:S(2)}, u32[]{:S(2)}) async-start(bf16[3,250,4096]{1,0,2:T(4,128)(2,1)} %copy.11), calls=%async_computation | async-start | bytes 16777216 | tf_op jit(solution)/shard_map/all_to_all | solution.py:82
  31.3 110.5 %multiply_convert_fusion.1 = (bf16[16000,320]{1,0:T(8,128)(2,1)}, bf16[16000,320]{1,0:T(8,128)(2,1)}) fusion(f32[16000]{0:T(1024)S(1)} %multiply_subtract_fusion, s32[320]{0:T(512)S(1)} %iota_add_fusion.1), kind=kLoop, calls=%fused_computation.23 | loop fusion | flops 71680000 | bytes 20545280 | tf_op jit(solution)/shard_map/convert.8
  141.8 4.3 copy.12
  146.0 6.3 %copy.13 = bf16[3,64,250,64]{2,1,3,0:T(8,128)(2,1)} copy(bf16[3,64,250,64]{2,3,1,0:T(8,128)(2,1)S(1)} %bitcast.96) | data formatting | bytes 12288000 | tf_op jit(solution)/shard_map/all_to_all | solution.py:82
  152.3 12.4 %all_to_all.16 = bf16[3,16000,64]{1,2,0:T(8,128)(2,1)} reshape(bf16[3,64,250,64]{2,1,3,0:T(8,128)(2,1)} %copy.13) | data formatting | bytes 12288000 | tf_op jit(solution)/shard_map/all_to_all | solution.py:82
  164.8 14.0 %fusion.17 = f32[640,192]{0,1:S(1)} fusion(bf16[16000,192]{0,1:T(8,128)(2,1)} %bitcast.99, bf16[16000,320]{1,0:T(8,128)(2,1)} %get-tuple-element.70, bf16[16000,320]{1,0:T(8,128)(2,1)} %get-tuple-element.69), kind=kOutput, calls=%fused_computation.28 | convolution fusion | flops 3973120000 | bytes 27115520
  181.4 4.7 multiply_convert_fusion.3
  187.2 112.5 %all-gather.2.cloned.1.call-done = bf16[3,4096,512]{2,1,0:T(8,128)(2,1)} async-done(((bf16[3,64,512]{2,1,0:T(8,128)(2,1)}), bf16[3,4096,512]{2,1,0:T(8,128)(2,1)}) %all-gather.2.cloned.1.call-update) | async-done | bytes 12582928 | tf_op jit(solution)/shard_map/all_gather | solution.py:96
  299.8 8.8 %while.20 = (s32[]{:T(128)}, bf16[4,3,64,512]{3,2,1,0:T(8,128)(2,1)S(1)}, s32[4]{0:T(128)S(1)}, bf16[3,4096,512]{2,1,0:T(8,128)(2,1)}, s32[]{:T(128)}, /*index=5*/s32[1]{0:T(128)}, s32[]{:T(128)}, s32[]{:T(128)}) while((s32[]{:T(128)}, bf16[4,3,64,512]{3,2,1,0:T(8,128)(2,1)S(1)}, s32[4]{0:T(128)S(1)}, bf16[3,4096,512]{2,1,0:T(8,128)(2,1)}, ...), condition=%wide.region_1.2_spmd, body=%wide.region_0.1_spmd.sunk | while | flops 6 | bytes 393367 | solution.py:101
  308.6 1.4 copy.14
  310.0 81.5 %while.21 = (s32[]{:T(128)}, bf16[2,4096,1024]{2,1,0:T(8,128)(2,1)}, bf16[2,2,3,64,512]{3,2,4,1,0:T(4,128)(2,1)S(1)}, bf16[512,1024]{1,0:T(8,128)(2,1)}, s32[]{:T(128)}, /*index=5*/s32[]{:T(128)}, s32[]{}) while((s32[]{:T(128)}, bf16[2,4096,1024]{2,1,0:T(8,128)(2,1)}, bf16[2,2,3,64,512]{3,2,4,1,0:T(4,128)(2,1)S(1)}, ...), condition=%wide.region_3.4_spmd, body=%wide.region_2.3_spmd.sunk | while | flops 4326424576 | bytes 79823624 | solution.py:112
  312.8 3.5 fusion.93
  317.8 3.5 fusion.89
  321.3 8.5 %pad_maximum_fusion.4 = bf16[64,64,512]{0,1,2:T(8,128)(2,1)} fusion(bf16[64,64,256]{0,1,2:T(8,128)(2,1)} %fusion.89, bf16[64,64,256]{0,1,2:T(8,128)(2,1)} %fusion.93), kind=kLoop, calls=%fused_computation.2.clone.1 | loop fusion | flops 2097152 | bytes 8388608 | tf_op jit(solution)/shard_map/while/body/eval_jaxpr/concatenate | solution.py:68
  329.8 12.2 %copy.16 = bf16[64,64,512]{2,1,0:T(8,128)(2,1)} copy(bf16[64,64,512]{0,1,2:T(8,128)(2,1)} %pad_maximum_fusion.4) | data formatting | bytes 8388608 | tf_op jit(solution)/shard_map/while/body/eval_jaxpr/concatenate | solution.py:68
  341.9 9.0 %bitcast_dynamic-update-slice_fusion.5 = bf16[2,4096,1024]{2,1,0:T(8,128)(2,1)} fusion(bf16[2,4096,1024]{2,1,0:T(8,128)(2,1)} %get-tuple-element.155, s32[]{:T(128)} %get-tuple-element.154, bf16[4096,512]{1,0:T(8,128)(2,1)} %bitcast.95, bf16[512,1024]{1,0:T(8,128)(2,1)S(1)} %copy-done.4), kind=kOutput, calls=%fused_computation.1.clone.1 | convolution fusion | flops 4294967296 | bytes 22020608 | tf_op jit(solution)/shard_map/while/body/eval_jaxpr/dot_general | solution.py:106
  352.0 1.3 fusion.91
  353.4 3.5 fusion.93
  358.5 3.5 fusion.89
  362.0 8.5 %pad_maximum_fusion.4 = bf16[64,64,512]{0,1,2:T(8,128)(2,1)} fusion(bf16[64,64,256]{0,1,2:T(8,128)(2,1)} %fusion.89, bf16[64,64,256]{0,1,2:T(8,128)(2,1)} %fusion.93), kind=kLoop, calls=%fused_computation.2.clone.1 | loop fusion | flops 2097152 | bytes 8388608 | tf_op jit(solution)/shard_map/while/body/eval_jaxpr/concatenate | solution.py:68
  370.5 12.2 %copy.16 = bf16[64,64,512]{2,1,0:T(8,128)(2,1)} copy(bf16[64,64,512]{0,1,2:T(8,128)(2,1)} %pad_maximum_fusion.4) | data formatting | bytes 8388608 | tf_op jit(solution)/shard_map/while/body/eval_jaxpr/concatenate | solution.py:68
  382.6 8.9 %bitcast_dynamic-update-slice_fusion.5 = bf16[2,4096,1024]{2,1,0:T(8,128)(2,1)} fusion(bf16[2,4096,1024]{2,1,0:T(8,128)(2,1)} %get-tuple-element.155, s32[]{:T(128)} %get-tuple-element.154, bf16[4096,512]{1,0:T(8,128)(2,1)} %bitcast.95, bf16[512,1024]{1,0:T(8,128)(2,1)S(1)} %copy-done.4), kind=kOutput, calls=%fused_computation.1.clone.1 | convolution fusion | flops 4294967296 | bytes 22020608 | tf_op jit(solution)/shard_map/while/body/eval_jaxpr/dot_general | solution.py:106
  391.5 192.0 %reduce-scatter.2.cloned.1.call-done = bf16[1,1,64,64,1024]{4,3,2,1,0:T(8,128)(2,1)} async-done(((bf16[2,1,64,64,1024]{4,3,2,1,0:T(8,128)(2,1)}), bf16[1,1,64,64,1024]{4,3,2,1,0:T(8,128)(2,1)}) %reduce-scatter.2.cloned.1.call-update) | async-done | bytes 8388624 | tf_op jit(solution)/shard_map/reduce_scatter | solution.py:113
  (65 shorter events, 17.0 us)
Async XLA Ops:
  19.6 11.3 %copy-start.6 = (s32[64]{0:T(128)S(1)}, s32[64]{0:T(128)}, u32[]{:S(2)}) copy-start(s32[64]{0:T(128)} %param.8) | copy-start | bytes 772
  19.6 122.2 %all-to-all-start = ((bf16[3,250,4096]{1,0,2:T(4,128)(2,1)}), bf16[3,250,4096]{1,0,2:T(4,128)(2,1)}, u32[]{:S(2)}, u32[]{:S(2)}) async-start(bf16[3,250,4096]{1,0,2:T(4,128)(2,1)} %copy.11), calls=%async_computation | async-start | bytes 16777216 | tf_op jit(solution)/shard_map/all_to_all | solution.py:82
  30.8 268.9 %all-gather.2.cloned.1.call-start = ((), (), s32[]{:S(2)}) async-start(), calls=%async_computation.2 | async-start | bytes 12779520 | tf_op jit(solution)/shard_map/all_gather | solution.py:96
  164.8 15.9 %copy-start.5 = (s32[2,1,2]{2,1,0:T(1,128)S(1)}, s32[2,1,2]{2,1,0:T(1,128)}, u32[]{:S(2)}) copy-start(s32[2,1,2]{2,1,0:T(1,128)} %param.9) | copy-start | bytes 52
  180.1 403.4 %reduce-scatter.2.cloned.1.call-start = ((), (), s32[]{:S(2)}) async-start(), calls=%async_computation.3 | async-start | bytes 25165824 | tf_op jit(solution)/shard_map/reduce_scatter | solution.py:113
  310.4 0.8 copy-start
  311.3 1.3 copy-start.1
  312.7 3.5 copy-start.2
  316.4 1.3 copy-start.3
  329.8 12.2 %copy-start.4 = (bf16[512,1024]{1,0:T(8,128)(2,1)S(1)}, bf16[512,1024]{1,0:T(8,128)(2,1)}, u32[]{:S(2)}) copy-start(bf16[512,1024]{1,0:T(8,128)(2,1)} %get-tuple-element.164) | copy-start | bytes 3145732 | tf_op jit(solution)/shard_map/while
  351.1 0.8 copy-start
  352.0 1.3 copy-start.1
  353.4 3.5 copy-start.2
  357.0 1.3 copy-start.3
  370.5 12.2 %copy-start.4 = (bf16[512,1024]{1,0:T(8,128)(2,1)S(1)}, bf16[512,1024]{1,0:T(8,128)(2,1)}, u32[]{:S(2)}) copy-start(bf16[512,1024]{1,0:T(8,128)(2,1)} %get-tuple-element.164) | copy-start | bytes 3145732 | tf_op jit(solution)/shard_map/while
Sparse Core Ops, SparseCore 0:
  180.2 119.4 all-gather.1
  391.7 191.7 reduce-scatter.1
where the time goes:
time: 592 us; the launch traced here: 590 us
  waiting for transfers between devices  305 us (52%)
  other arithmetic  135 us (23%)
  local copies, waits for them, and re-layouts  71.2 us (12%)
  matrix products  51.7 us (9%)
  between operations  13.5 us (2%)
  starting transfers between devices  11.3 us (2%)
    reduce_scatter x1, waiting for transfers between devices, per_device(): lax.psum_scatter(lagged.reshape(1 * lax.axis_size('tm'), pairs_here, CB,...  192 us
    another operation x2, other arithmetic  115 us
    all_gather x1, waiting for transfers between devices, per_device(): everyone = lax.all_gather(spectra, 'chan', axis=1, tiled=True)  113 us
    concatenate x2, local copies, waits for them, and re-layouts, cross_spectrum(): jnp.concatenate([real_sum, imag_sum], -1).reshape(CB * CB, 2 * F)  24.3 us
    all_to_all x3, local copies, waits for them, and re-layouts, per_device(): lax.all_to_all(strain, 'chan', split_axis=2, concat_axis=1, tiled=True)  23 us
    dot_general x2, matrix products, pair_lags(): jnp.dot(cross_spectrum(pair_blocks[0], pair_blocks[1]), backward, preferr...  17.9 us
    concatenate x2, other arithmetic, cross_spectrum(): jnp.concatenate([real_sum, imag_sum], -1).reshape(CB * CB, 2 * F)  17 us
    unnamed x1, matrix products  14 us
  transfers between devices with their start and end apart: 3, of which 2 were waited for; matrix products, arithmetic and copies ran while one was open for 20% of the time, Pallas kernels for 0%

commit v1 on v0

v1 whole, which is shorter than its diff:
```python
import functools
import math

import jax
import jax.numpy as jnp
import numpy as np
from jax import lax
from jax.experimental import pallas as pl
from jax.experimental.pallas import tpu as pltpu
from jax.sharding import PartitionSpec as P

CB = 64
W = 16000
NB = 64
WIN_DEV = 3
NWIN = 6
K0 = 64
F = 256
HALF = 32
WIDTH = F + 2 * HALF
LAGS = 1024
SAMPLES = W // NB
RANK = 24
UNITS = 5
ROWS = 8 * UNITS
CHUNK = 24
LANES = 128
TILES = CB * NB // LANES
EPS = 1e-05
F32 = jnp.float32
BF16 = jnp.bfloat16


def time_basis():
    places = np.arange(SAMPLES)
    main = ((SAMPLES - 1 - 2 * places) / 2.0) ** 2 * np.cos(2 * np.pi * (K0 - HALF + WIDTH) / W)
    side = places[1:] * (SAMPLES - places[1:]) / 2.0
    _, vectors = np.linalg.eigh(np.diag(main) + np.diag(side, 1) + np.diag(side, -1))
    basis = vectors[:, ::-1][:, :RANK]
    mid = SAMPLES // 2
    centre = np.where(np.arange(RANK) % 2 == 0, basis[mid] + basis[mid - 1], basis[mid] - basis[mid - 1])
    return basis * np.sign(centre)[None, :]


def block_tables(basis):
    local = np.arange(SAMPLES)
    bins = np.arange(K0 - HALF, K0 - HALF + WIDTH)
    out = np.empty((2 * WIDTH, RANK // 8, NB, 8))
    for block in range(NB):
        index = ((block * SAMPLES + local)[:, None] * bins[None, :]) % W
        angles = 2 * np.pi / W * index
        table = np.concatenate([np.cos(angles), -np.sin(angles)], 1)
        out[:, :, block, :] = (table.T @ basis).reshape(2 * WIDTH, RANK // 8, 8)
    return out.reshape(2 * WIDTH, RANK * NB)


def lag_table():
    freqs = (K0 + np.arange(F))[:, None]
    steps = (np.arange(LAGS) - LAGS // 2)[None, :]
    angles = 2 * np.pi / W * (freqs * steps % W)
    factor = 1.0 / math.sqrt(WIN_DEV * F)
    return np.concatenate([np.cos(angles) * factor, -np.sin(angles) * factor], 0)


def smoothing_ones():
    rows = np.arange(F)[:, None]
    cols = np.arange(WIDTH)[None, :]
    return (np.abs(cols - rows - HALF) <= HALF).astype(np.float32)


def band_weights():
    freqs = np.arange(F) + 0.5
    ramp = np.minimum(freqs, F - freqs) / (F / 4.0)
    return np.where(ramp < 1.0, 0.5 - 0.5 * np.cos(np.pi * ramp), 1.0)


def project_kernel(steps, pairs_ref, live_ref, basis_ref, x_ref, o_ref, z_ref):
    step = pl.program_id(0)
    per = TILES // steps
    block = lax.axis_index("chan")
    place = lax.broadcasted_iota(jnp.int32, (1, SAMPLES), 1) + block * SAMPLES
    hann = 0.5 - 0.5 * jnp.cos((2.0 * math.pi / W) * place.astype(F32))
    table = (basis_ref[...] * hann).astype(BF16)
    for win in range(WIN_DEV):
        coef = jnp.dot(table, x_ref[win], preferred_element_type=F32)
        for tile in range(per):
            at = 2 * (step * per + tile)
            part = coef[:, tile * LANES : (tile + 1) * LANES]
            unit = [part[8 * s : 8 * s + 8] for s in range(3)]
            if win < 2:
                for s in range(3):
                    z_ref[s, at + win] = unit[s]
            else:
                z_ref[3, at] = unit[0]
                z_ref[3, at + 1] = unit[1]
                z_ref[4, at] = unit[2]
                z_ref[4, at + 1] = jnp.zeros((8, LANES), F32)

    @pl.when(step == steps - 1)
    def _():
        lane = lax.broadcasted_iota(jnp.int32, (8, LANES), 1)
        extra = jnp.zeros((8, LANES), F32)
        for s in range(2):
            for side in range(2):
                value = pairs_ref[s, 0, side].astype(F32)
                extra = jnp.where(lane == 1 + 4 * s + 2 * side, value, extra)
        for u in range(UNITS):
            z = [z_ref[u, v] for v in range(CB)]
            for bit in range(6):
                stride = 1 << bit
                high = ((lane >> bit) & 1) == 1
                for v in range(CB):
                    if v & stride:
                        continue
                    x0, x1 = z[v], z[v | stride]
                    z[v] = jnp.where(high, pltpu.roll(x1, stride, 1), x0)
                    z[v | stride] = jnp.where(high, x1, pltpu.roll(x0, LANES - stride, 1))
            if u == UNITS - 1:
                for v in range(CB):
                    z[v] = z[v] + jnp.where(lane == 9, live_ref[v].astype(F32), extra)
            for v in range(CB):
                z_ref[u, v] = z[v]
        for v in range(CB):
            o_ref[v] = jnp.concatenate([z_ref[u, v] for u in range(UNITS)], 0).astype(BF16)


def project(strain, live_mask, block_pairs, basis):
    steps = 4
    width = CB * NB // steps
    return pl.pallas_call(
        functools.partial(project_kernel, steps),
        grid=(steps,),
        out_shape=jax.ShapeDtypeStruct((CB, ROWS, LANES), BF16),
        in_specs=[
            pl.BlockSpec(memory_space=pltpu.SMEM),
            pl.BlockSpec(memory_space=pltpu.SMEM),
            pl.BlockSpec((RANK, SAMPLES), lambda g: (0, 0)),
            pl.BlockSpec((WIN_DEV, SAMPLES, width), lambda g: (0, 0, g)),
        ],
        out_specs=pl.BlockSpec((CB, ROWS, LANES), lambda g: (0, 0, 0)),
        scratch_shapes=[pltpu.VMEM((UNITS, CB, 8, LANES), F32)],
        compiler_params=pltpu.CompilerParams(vmem_limit_bytes=24 * 2**20),
        cost_estimate=pl.CostEstimate(flops=400_000_000, bytes_accessed=7_000_000, transcendentals=0),
        name="project",
    )(block_pairs, live_mask, basis, strain)


def slot(index):
    return ((index & 1) << 5) | (index >> 1)


def whiten_kernel(r_ref, table_ref, ones_ref, taper_ref, o_ref, extra_ref, index_ref, small_ref, spec_ref, rows_ref, sem):
    received = r_ref[...].astype(F32)
    unit = [received[:, 8 * u : 8 * u + 8].reshape(8 * NB, LANES) for u in range(UNITS)]
    extra_ref[...] = unit[4]
    index_ref[...] = extra_ref[pl.ds(0, NB, stride=8), :].astype(jnp.int32)
    copy = pltpu.make_async_copy(index_ref, small_ref, sem)
    copy.start()
    even = extra_ref[pl.ds(0, NB // 2, stride=16), :]
    odd = extra_ref[pl.ds(8, NB // 2, stride=16), :]
    live = jnp.concatenate([even, odd], 0)[:, 9:10]
    left = jnp.concatenate(unit[:3], 0)
    right = jnp.concatenate([unit[3], pltpu.roll(unit[3], LANES - 1, 1), unit[4]], 0)
    operand = jnp.concatenate([left, right], 1).astype(BF16)
    raw = jnp.dot(table_ref[...], operand, preferred_element_type=F32)
    real, imag = raw[:WIDTH], raw[WIDTH:]
    magnitude = jnp.sqrt(real * real + imag * imag)
    ones = ones_ref[...]
    total = jnp.zeros((F, 2 * LANES), F32)
    rest = magnitude
    for _ in range(3):
        piece = rest.astype(BF16)
        rest = rest - piece.astype(F32)
        total = total + jnp.dot(ones, piece, preferred_element_type=F32)
    weight = 1.0 / (total * (1.0 / (2 * HALF + 1)) + EPS)
    for tile in range(2 * F // LANES):
        part = real if tile < F // LANES else imag
        start = tile * LANES % F
        picked = part[HALF + start : HALF + start + LANES] * weight[start : start + LANES]
        spec_ref[tile] = picked.T
    for win, start in enumerate((0, 1, LANES)):
        for tile in range(2 * F // LANES):
            cols = slice(tile * LANES, (tile + 1) * LANES)
            value = spec_ref[tile, pl.ds(start, NB, stride=2), :] * taper_ref[:, cols] * live
            rows_ref[pl.ds(win * 4 + tile, NB, stride=16), :] = value
            if win == 2:
                rows_ref[pl.ds(12 + tile, NB, stride=16), :] = value
    copy.wait()
    low = lax.broadcasted_iota(jnp.int32, (8, LANES), 0) < 4

    @pl.loop(0, NB)
    def _(device):
        for s in range(2):
            first = slot(small_ref[device, 1 + 4 * s])
            second = slot(small_ref[device, 3 + 4 * s])
            a = rows_ref[pl.ds(pl.multiple_of(first * 16, 16), 16), :]
            b = rows_ref[pl.ds(pl.multiple_of(second * 16, 16), 16), :]
            chunk = jnp.concatenate([a[:8], jnp.where(low, a[8:], b[8:]), b[:8]], 0)
            o_ref[s * NB + device] = chunk.astype(BF16)


def whiten(received, table, ones, taper):
    return pl.pallas_call(
        whiten_kernel,
        out_shape=jax.ShapeDtypeStruct((2 * NB, CHUNK, LANES), BF16),
        in_specs=[pl.BlockSpec(memory_space=pltpu.VMEM)] * 4,
        out_specs=pl.BlockSpec(memory_space=pltpu.VMEM),
        scratch_shapes=[
            pltpu.VMEM((8 * NB, LANES), F32),
            pltpu.VMEM((NB, LANES), jnp.int32),
            pltpu.SMEM((NB, LANES), jnp.int32),
            pltpu.VMEM((2 * F // LANES, 2 * LANES, LANES), F32),
            pltpu.VMEM((16 * NB, LANES), F32),
            pltpu.SemaphoreType.DMA,
        ],
        compiler_params=pltpu.CompilerParams(vmem_limit_bytes=24 * 2**20),
        cost_estimate=pl.CostEstimate(flops=600_000_000, bytes_accessed=4_000_000, transcendentals=100_000),
        name="whiten",
    )(received, table, ones, taper)


GROUP = 8


def lags_kernel(g_ref, back_ref, o_ref, flat_ref, a_ref, b_ref, cross_ref):
    step = pl.program_id(0)

    @pl.when(step == 0)
    def _():
        flat_ref[...] = g_ref[...].astype(F32).reshape(2 * CB * CHUNK, LANES)
        for group in range(2):
            for win in range(WIN_DEV):
                for tile in range(2 * F // LANES):
                    cols = slice(tile * LANES, (tile + 1) * LANES)
                    at = win * 4 + tile
                    places = (at, 12 + tile if win == 2 else 16 + at)
                    for ref, place in zip((a_ref, b_ref), places):
                        start = group * CB * CHUNK + place
                        ref[group * WIN_DEV + win, :, cols] = flat_ref[pl.ds(start, CB, stride=CHUNK), :]

    rows = pl.ds(pl.multiple_of(step * GROUP, GROUP), GROUP)
    for k in range(GROUP):
        for tile in range(F // LANES):
            re = slice(tile * LANES, (tile + 1) * LANES)
            im = slice(F + tile * LANES, F + (tile + 1) * LANES)
            real = jnp.zeros((CB, LANES), F32)
            imag = jnp.zeros((CB, LANES), F32)
            for win in range(NWIN):
                ar = a_ref[win, rows, re][k : k + 1]
                ai = a_ref[win, rows, im][k : k + 1]
                br = b_ref[win, :, re]
                bi = b_ref[win, :, im]
                real = real + (ar * br + ai * bi)
                imag = imag + (ai * br - ar * bi)
            cross_ref[k * CB : (k + 1) * CB, re] = real.astype(BF16)
            cross_ref[k * CB : (k + 1) * CB, im] = imag.astype(BF16)
    lags = jnp.dot(cross_ref[...], back_ref[...], preferred_element_type=F32)
    o_ref[...] = lags.astype(BF16).reshape(GROUP, CB, LAGS)


def pair_lags(gathered, back):
    return pl.pallas_call(
        lags_kernel,
        grid=(CB // GROUP,),
        out_shape=jax.ShapeDtypeStruct((CB, CB, LAGS), BF16),
        in_specs=[
            pl.BlockSpec((2 * CB, CHUNK, LANES), lambda g: (0, 0, 0)),
            pl.BlockSpec((2 * F, LAGS), lambda g: (0, 0)),
        ],
        out_specs=pl.BlockSpec((GROUP, CB, LAGS), lambda g: (g, 0, 0)),
        scratch_shapes=[
            pltpu.VMEM((2 * CB * CHUNK, LANES), F32),
            pltpu.VMEM((NWIN, CB, 2 * F), F32),
            pltpu.VMEM((NWIN, CB, 2 * F), F32),
            pltpu.VMEM((GROUP * CB, 2 * F), BF16),
        ],
        compiler_params=pltpu.CompilerParams(vmem_limit_bytes=32 * 2**20),
        cost_estimate=pl.CostEstimate(flops=4_400_000_000, bytes_accessed=12_000_000, transcendentals=0),
        name="pair_lags",
    )(gathered, back)


def solution(mesh):
    basis_np = time_basis()
    table_np = block_tables(basis_np).astype(jnp.bfloat16)
    back_np = lag_table().astype(jnp.bfloat16)

    def per_device(strain, live_mask, block_pairs):
        basis = jnp.asarray(basis_np.T.astype(np.float32))
        ones = jnp.asarray(smoothing_ones().astype(jnp.bfloat16))
        taper = jnp.asarray(np.tile(band_weights(), 2)[None, :].astype(np.float32))
        coefs = project(strain, live_mask, block_pairs, basis)
        with jax.named_scope("channels_exchange"):
            received = lax.all_to_all(coefs, "chan", 0, 0, tiled=True)
        chosen = whiten(received, jnp.asarray(table_np), ones, taper)
        with jax.named_scope("pairs_exchange"):
            gathered = lax.all_to_all(chosen, ("tm", "chan"), 0, 0, tiled=True)
        return pair_lags(gathered, jnp.asarray(back_np)).reshape(1, 1, CB, CB, LAGS)

    in_specs = (P("tm", "chan", None), P("chan"), P(None, "chan", None))
    out_specs = P("tm", "chan", None, None, None)
    return jax.shard_map(per_device, mesh=mesh, in_specs=in_specs, out_specs=out_specs, check_vma=False)
```

time: 592 us -> 73.5 us (0.12)
  waiting for transfers between devices: 305 us -> 0 us
  other arithmetic: 135 us -> 0 us
  local copies, waits for them, and re-layouts: 71.2 us -> 4.88 us
  matrix products: 51.7 us -> 0 us
  blocking collectives: 0 us -> 47 us
  Pallas kernels: 0 us -> 21.4 us
  between operations: 13.5 us -> 0.03 us
  starting transfers between devices: 11.3 us -> 0 us
    reduce_scatter x1 -> x0, waiting for transfers between devices: 192 us -> none  [per_device(): lax.psum_scatter(lagged.reshape(1 * lax.axis_size('tm'), pairs_here, CB,...]
    another operation x2 -> x0, other arithmetic: 115 us -> none
    all_gather x1 -> x0, waiting for transfers between devices: 113 us -> none  [per_device(): everyone = lax.all_gather(spectra, 'chan', axis=1, tiled=True)]
    all_to_all x0 -> x2, blocking collectives: none -> 47 us  [the longest x1 24.5 us: per_device(): received = lax.all_to_all(coefs, 'chan', 0, 0, tiled=True)]
    dot_general x11 -> x0, matrix products: 37.7 us -> none  [the longest x2 17.9 us: pair_lags(): jnp.dot(cross_spectrum(pair_blocks[0], pair_blocks[1]), backward, preferr...]
    concatenate x2 -> x0, local copies, waits for them, and re-layouts: 24.3 us -> none  [cross_spectrum(): jnp.concatenate([real_sum, imag_sum], -1).reshape(CB * CB, 2 * F)]
    all_to_all x3 -> x0, local copies, waits for them, and re-layouts: 23 us -> none  [per_device(): lax.all_to_all(strain, 'chan', split_axis=2, concat_axis=1, tiled=True)]
    pallas_call x0 -> x3, Pallas kernels: none -> 21.4 us  [the longest x1 12.8 us: pair_lags(): pl.pallas_call(lags_kernel, grid=(CB // GROUP,), out_shape=jax.ShapeDtype...]
  transfers between devices with their start and end apart: 3 -> 0, of which waited for: 2 -> 0; matrix products, arithmetic and copies ran while one was open for 20% -> 0% of each run, Pallas kernels for 0% -> 0%
where the time goes in v1:
time: 73.5 us; the launch traced here: 73.3 us
  blocking collectives  47 us (64%)
  Pallas kernels  21.4 us (29%)
  local copies, waits for them, and re-layouts  4.88 us (7%)
    all_to_all x1, blocking collectives, per_device(): received = lax.all_to_all(coefs, 'chan', 0, 0, tiled=True)  24.5 us
    all_to_all x1, blocking collectives, per_device(): gathered = lax.all_to_all(chosen, ('tm', 'chan'), 0, 0, tiled=True)  22.4 us
    pallas_call x1, Pallas kernels, pair_lags(): pl.pallas_call(lags_kernel, grid=(CB // GROUP,), out_shape=jax.ShapeDtype...  12.8 us
    pallas_call x1, Pallas kernels, project(): pl.pallas_call(functools.partial(project_kernel, steps), grid=(steps,), o...  4.98 us
    unnamed x16, local copies, waits for them, and re-layouts  4.88 us
    pallas_call x1, Pallas kernels, whiten(): pl.pallas_call(whiten_kernel, out_shape=jax.ShapeDtypeStruct((2 * NB, CHU...  3.57 us

profile of v1, /device:TPU:1, one launch (start us, length us, event | category | flops | bytes accessed | tf_op | source)
XLA Modules:
  0.0 73.3 jit_solution(16698654637299638101)
XLA Ops:
  0.0 0.0 copy-start.4
  0.0 0.0 copy-start
  0.0 2.8 %copy-done = bf16[3,250,4096]{2,1,0:T(8,128)(2,1)S(1)} copy-done((bf16[3,250,4096]{2,1,0:T(8,128)(2,1)S(1)}, bf16[3,250,4096]{2,1,0:T(8,128)(2,1)}, u32[]{:S(2)}) %copy-start) | copy-done | bytes 6144024
  2.8 0.0 copy-start.3
  2.8 0.7 %copy-done.3 = f32[24,250]{1,0:T(8,128)S(1)} copy-done((f32[24,250]{1,0:T(8,128)S(1)}, f32[24,250]{1,0:T(8,128)}, u32[]{:S(2)}) %copy-start.3) | copy-done | bytes 24024
  3.5 0.0 copy-start.5
  3.5 0.7 copy-done.5
  4.2 0.0 copy-start.6
  4.2 0.7 copy-done.6
  4.9 0.0 copy-start.1
  4.9 0.0 copy-start.2
  4.9 0.0 copy-start.7
  4.9 5.0 %project.1 = bf16[64,40,128]{2,1,0:T(8,128)(2,1)S(1)} custom-call(s32[2,1,2]{2,1,0:T(1,128)S(1)} %copy-done.5, s32[64]{0:T(128)S(1)} %copy-done.6, f32[24,250]{1,0:T(8,128)S(1)} %copy-done.3, bf16[3,250,4096]{2,1,0:T(8,128)(2,1)S(1)} %copy-done), custom_call_target="tpu_custom_call" | custom-call | flops 400000000 | bytes 7000000 | tf_op jit(solution)/shard_map/project/pallas_call | solution.py:130
  9.9 24.5 %all_to_all.10.r_ref = bf16[64,40,128]{2,1,0:T(8,128)(2,1)S(1)} all-to-all(bf16[64,40,128]{2,1,0:T(8,128)(2,1)S(1)} %project.1), channel_id=1, replica_groups=mesh['tm'=2,'chan'=64] {'chan'}, dimensions={0} | all-to-all | bytes 1310720 | tf_op jit(solution)/shard_map/channels_exchange/all_to_all | solution.py:294
  34.4 0.0 copy-done.4
  34.4 0.0 copy-done.1
  34.4 0.0 copy-done.2
  34.4 3.6 %whiten.1 = bf16[128,24,128]{2,1,0:T(8,128)(2,1)S(1)} custom-call(bf16[64,40,128]{2,1,0:T(8,128)(2,1)S(1)} %all_to_all.10.r_ref, bf16[640,1536]{1,0:T(8,128)(2,1)S(1)} %copy-done.1, bf16[256,320]{1,0:T(8,128)(2,1)S(1)} %copy-done.2, f32[1,512]{1,0:T(1,128)S(1)} %copy-done.4), custom_call_target="tpu_custom_call" | custom-call | flops 600000000 | bytes 4000000 | tf_op jit(solution)/shard_map/whiten/pallas_call | solution.py:203
  38.0 22.4 %all_to_all.11.g_ref = bf16[128,24,128]{2,1,0:T(8,128)(2,1)S(1)} all-to-all(bf16[128,24,128]{2,1,0:T(8,128)(2,1)S(1)} %whiten.1), channel_id=1, replica_groups=mesh['tm'=2,'chan'=64] {'tm','chan'}, dimensions={0} | all-to-all | bytes 1572864 | tf_op jit(solution)/shard_map/pairs_exchange/all_to_all | solution.py:297
  60.4 0.0 copy-done.7
  60.4 12.8 %pair_lags.1 = bf16[64,64,1024]{2,1,0:T(8,128)(2,1)} custom-call(bf16[128,24,128]{2,1,0:T(8,128)(2,1)S(1)} %all_to_all.11.g_ref, bf16[512,1024]{1,0:T(8,128)(2,1)S(1)} %copy-done.7), custom_call_target="tpu_custom_call" | custom-call | flops 4400000000 | bytes 12000000 | tf_op jit(solution)/shard_map/pair_lags/pallas_call | solution.py:262
Async XLA Ops:
  0.0 34.4 %copy-start.4 = (f32[1,512]{1,0:T(1,128)S(1)}, f32[1,512]{1,0:T(1,128)}, u32[]{:S(2)}) copy-start(f32[1,512]{1,0:T(1,128)} %constant.12.clone.taper_ref) | copy-start | bytes 6148
  0.0 2.8 %copy-start = (bf16[3,250,4096]{2,1,0:T(8,128)(2,1)S(1)}, bf16[3,250,4096]{2,1,0:T(8,128)(2,1)}, u32[]{:S(2)}) copy-start(bf16[3,250,4096]{2,1,0:T(8,128)(2,1)} %x_ref.1) | copy-start | bytes 18432004
  2.8 0.7 %copy-start.3 = (f32[24,250]{1,0:T(8,128)S(1)}, f32[24,250]{1,0:T(8,128)}, u32[]{:S(2)}) copy-start(f32[24,250]{1,0:T(8,128)} %constant.10.clone.basis_ref) | copy-start | bytes 72004
  3.5 0.7 copy-start.5
  4.2 0.7 copy-start.6
  4.9 29.5 %copy-start.1 = (bf16[640,1536]{1,0:T(8,128)(2,1)S(1)}, bf16[640,1536]{1,0:T(8,128)(2,1)}, u32[]{:S(2)}) copy-start(bf16[640,1536]{1,0:T(8,128)(2,1)} %constant.13.clone.table_ref) | copy-start | bytes 5898244
  4.9 29.5 %copy-start.2 = (bf16[256,320]{1,0:T(8,128)(2,1)S(1)}, bf16[256,320]{1,0:T(8,128)(2,1)}, u32[]{:S(2)}) copy-start(bf16[256,320]{1,0:T(8,128)(2,1)} %constant.11.clone.ones_ref) | copy-start | bytes 491524
  4.9 55.6 %copy-start.7 = (bf16[512,1024]{1,0:T(8,128)(2,1)S(1)}, bf16[512,1024]{1,0:T(8,128)(2,1)}, u32[]{:S(2)}) copy-start(bf16[512,1024]{1,0:T(8,128)(2,1)} %constant.14.clone.back_ref) | copy-start | bytes 3145732

commit v2 on v1

--- a/solution.py
+++ b/solution.py
@@ -74,72 +74,100 @@
     return np.where(ramp < 1.0, 0.5 - 0.5 * np.cos(np.pi * ramp), 1.0)
 
 
-def project_kernel(steps, pairs_ref, live_ref, basis_ref, x_ref, o_ref, z_ref):
-    step = pl.program_id(0)
-    per = TILES // steps
+def project_kernel(parts, pairs_hbm, live_hbm, basis_ref, x_hbm, o_ref, x_ref, z_ref, pairs_ref, live_ref, sems):
+    per = TILES // parts
+    width = CB * NB // parts
+    copies = []
+    for c in range(parts):
+        cols = pl.ds(c * width, width)
+        copies.append(pltpu.make_async_copy(x_hbm.at[:, :, cols], x_ref.at[:, :, cols], sems.at[c]))
+    small = [
+        pltpu.make_async_copy(pairs_hbm, pairs_ref, sems.at[parts]),
+        pltpu.make_async_copy(live_hbm, live_ref, sems.at[parts + 1]),
+    ]
+    for copy in copies + small:
+        copy.start()
     block = lax.axis_index("chan")
     place = lax.broadcasted_iota(jnp.int32, (1, SAMPLES), 1) + block * SAMPLES
     hann = 0.5 - 0.5 * jnp.cos((2.0 * math.pi / W) * place.astype(F32))
     table = (basis_ref[...] * hann).astype(BF16)
-    for win in range(WIN_DEV):
-        coef = jnp.dot(table, x_ref[win], preferred_element_type=F32)
+    lane = lax.broadcasted_iota(jnp.int32, (16, LANES), 1)
+    masks = [((lane >> bit) & 1) == 1 for bit in range(6)]
+
+    def exchange(groups, bits, base):
+        for bit in bits:
+            stride, shift = 1 << (bit - base), 1 << bit
+            for v in range(len(groups[0])):
+                if v & stride:
+                    continue
+                for z in groups:
+                    x0, x1 = z[v], z[v | stride]
+                    z[v] = jnp.where(masks[bit], pltpu.roll(x1, shift, 1), x0)
+                    z[v | stride] = jnp.where(masks[bit], x1, pltpu.roll(x0, LANES - shift, 1))
+
+    count = 2 * per
+    local = count.bit_length() - 1
+    zero = jnp.zeros((8, LANES), BF16)
+    for c in range(parts):
+        copies[c].wait()
+        coef = [
+            jnp.dot(table, x_ref[win, :, c * width : (c + 1) * width], preferred_element_type=F32).astype(BF16)
+            for win in range(WIN_DEV)
+        ]
+        groups = [[], [], []]
         for tile in range(per):
-            at = 2 * (step * per + tile)
-            part = coef[:, tile * LANES : (tile + 1) * LANES]
-            unit = [part[8 * s : 8 * s + 8] for s in range(3)]
-            if win < 2:
-                for s in range(3):
-                    z_ref[s, at + win] = unit[s]
-            else:
-                z_ref[3, at] = unit[0]
-                z_ref[3, at + 1] = unit[1]
-                z_ref[4, at] = unit[2]
-                z_ref[4, at + 1] = jnp.zeros((8, LANES), F32)
-
-    @pl.when(step == steps - 1)
-    def _():
-        lane = lax.broadcasted_iota(jnp.int32, (8, LANES), 1)
-        extra = jnp.zeros((8, LANES), F32)
-        for s in range(2):
-            for side in range(2):
-                value = pairs_ref[s, 0, side].astype(F32)
-                extra = jnp.where(lane == 1 + 4 * s + 2 * side, value, extra)
-        for u in range(UNITS):
-            z = [z_ref[u, v] for v in range(CB)]
-            for bit in range(6):
-                stride = 1 << bit
-                high = ((lane >> bit) & 1) == 1
-                for v in range(CB):
-                    if v & stride:
-                        continue
-                    x0, x1 = z[v], z[v | stride]
-                    z[v] = jnp.where(high, pltpu.roll(x1, stride, 1), x0)
-                    z[v | stride] = jnp.where(high, x1, pltpu.roll(x0, LANES - stride, 1))
-            if u == UNITS - 1:
-                for v in range(CB):
-                    z[v] = z[v] + jnp.where(lane == 9, live_ref[v].astype(F32), extra)
-            for v in range(CB):
-                z_ref[u, v] = z[v]
-        for v in range(CB):
-            o_ref[v] = jnp.concatenate([z_ref[u, v] for u in range(UNITS)], 0).astype(BF16)
+            part = [coef[win][:, tile * LANES : (tile + 1) * LANES] for win in range(WIN_DEV)]
+            for h in range(2):
+                groups[0].append(part[h][:16])
+                groups[1].append(jnp.concatenate([part[h][16:], part[2][8 * h : 8 * h + 8]], 0))
+                groups[2].append(jnp.concatenate([part[2][16:] if h == 0 else zero, zero], 0))
+        exchange(groups, range(local), 0)
+        for k in range(3):
+            for v in range(count):
+                z_ref[k, c * count + v] = groups[k][v]
+    for copy in small:
+        copy.wait()
+    lane = lax.broadcasted_iota(jnp.int32, (8, LANES), 1)
+    extra = jnp.zeros((8, LANES), F32)
+    for s in range(2):
+        for side in range(2):
+            value = pairs_ref[s, 0, side].astype(F32)
+            extra = jnp.where(lane == 1 + 4 * s + 2 * side, value, extra)
+    for first in range(0, count, 4):
+        groups = [[z_ref[k, v + count * c] for c in range(parts)] for k in range(3) for v in range(first, first + 4)]
+        exchange(groups, range(local, 6), local)
+        for k in range(3):
+            for v in range(4):
+                for c in range(parts):
+                    slab = first + v + count * c
+                    value = groups[k * 4 + v][c]
+                    if k < 2:
+                        o_ref[slab, 16 * k : 16 * k + 16] = value
+                    else:
+                        added = jnp.where(lane == 9, live_ref[slab].astype(F32), extra)
+                        o_ref[slab, 32:40] = (value[:8].astype(F32) + added).astype(BF16)
 
 
 def project(strain, live_mask, block_pairs, basis):
-    steps = 4
-    width = CB * NB // steps
+    parts = 2
     return pl.pallas_call(
-        functools.partial(project_kernel, steps),
-        grid=(steps,),
+        functools.partial(project_kernel, parts),
         out_shape=jax.ShapeDtypeStruct((CB, ROWS, LANES), BF16),
         in_specs=[
-            pl.BlockSpec(memory_space=pltpu.SMEM),
-            pl.BlockSpec(memory_space=pltpu.SMEM),
-            pl.BlockSpec((RANK, SAMPLES), lambda g: (0, 0)),
-            pl.BlockSpec((WIN_DEV, SAMPLES, width), lambda g: (0, 0, g)),
+            pl.BlockSpec(memory_space=pltpu.HBM),
+            pl.BlockSpec(memory_space=pltpu.HBM),
+            pl.BlockSpec(memory_space=pltpu.VMEM),
+            pl.BlockSpec(memory_space=pltpu.HBM),
         ],
-        out_specs=pl.BlockSpec((CB, ROWS, LANES), lambda g: (0, 0, 0)),
-        scratch_shapes=[pltpu.VMEM((UNITS, CB, 8, LANES), F32)],
-        compiler_params=pltpu.CompilerParams(vmem_limit_bytes=24 * 2**20),
+        out_specs=pl.BlockSpec(memory_space=pltpu.VMEM),
+        scratch_shapes=[
+            pltpu.VMEM((WIN_DEV, SAMPLES, CB * NB), BF16),
+            pltpu.VMEM((3, CB, 16, LANES), BF16),
+            pltpu.SMEM((2, 1, 2), jnp.int32),
+            pltpu.SMEM((CB,), jnp.int32),
+            pltpu.SemaphoreType.DMA((parts + 2,)),
+        ],
+        compiler_params=pltpu.CompilerParams(vmem_limit_bytes=58 * 2**20),
         cost_estimate=pl.CostEstimate(flops=400_000_000, bytes_accessed=7_000_000, transcendentals=0),
         name="project",
     )(block_pairs, live_mask, basis, strain)
@@ -188,7 +216,7 @@
     copy.wait()
     low = lax.broadcasted_iota(jnp.int32, (8, LANES), 0) < 4
 
-    @pl.loop(0, NB)
+    @pl.loop(0, NB, unroll=8)
     def _(device):
         for s in range(2):
             first = slot(small_ref[device, 1 + 4 * s])
@@ -219,7 +247,7 @@
     )(received, table, ones, taper)
 
 
-GROUP = 8
+GROUP = 16
 
 
 def lags_kernel(g_ref, back_ref, o_ref, flat_ref, a_ref, b_ref, cross_ref):
@@ -236,24 +264,32 @@
                     places = (at, 12 + tile if win == 2 else 16 + at)
                     for ref, place in zip((a_ref, b_ref), places):
                         start = group * CB * CHUNK + place
-                        ref[group * WIN_DEV + win, :, cols] = flat_ref[pl.ds(start, CB, stride=CHUNK), :]
+                        value = flat_ref[pl.ds(start, CB, stride=CHUNK), :]
+                        ref[group * WIN_DEV + win, :, cols] = value.astype(ref.dtype)
 
     rows = pl.ds(pl.multiple_of(step * GROUP, GROUP), GROUP)
+
+    def spread(value):
+        value = jnp.broadcast_to(value, (16, LANES)).astype(BF16)
+        return jnp.concatenate([value] * (CB // 16), 0)
+
+    def total(terms):
+        return ((terms[0] + terms[1]) + (terms[2] + terms[3])) + (terms[4] + terms[5])
+
     for k in range(GROUP):
         for tile in range(F // LANES):
             re = slice(tile * LANES, (tile + 1) * LANES)
             im = slice(F + tile * LANES, F + (tile + 1) * LANES)
-            real = jnp.zeros((CB, LANES), F32)
-            imag = jnp.zeros((CB, LANES), F32)
+            real, imag = [], []
             for win in range(NWIN):
-                ar = a_ref[win, rows, re][k : k + 1]
-                ai = a_ref[win, rows, im][k : k + 1]
+                ar = spread(a_ref[win, rows, re][k : k + 1])
+                ai = spread(a_ref[win, rows, im][k : k + 1])
                 br = b_ref[win, :, re]
                 bi = b_ref[win, :, im]
-                real = real + (ar * br + ai * bi)
-                imag = imag + (ai * br - ar * bi)
-            cross_ref[k * CB : (k + 1) * CB, re] = real.astype(BF16)
-            cross_ref[k * CB : (k + 1) * CB, im] = imag.astype(BF16)
+                real.append(ar * br + ai * bi)
+                imag.append(ai * br - ar * bi)
+            cross_ref[k * CB : (k + 1) * CB, re] = total(real)
+            cross_ref[k * CB : (k + 1) * CB, im] = total(imag)
     lags = jnp.dot(cross_ref[...], back_ref[...], preferred_element_type=F32)
     o_ref[...] = lags.astype(BF16).reshape(GROUP, CB, LAGS)
 
@@ -263,15 +299,12 @@
         lags_kernel,
         grid=(CB // GROUP,),
         out_shape=jax.ShapeDtypeStruct((CB, CB, LAGS), BF16),
-        in_specs=[
-            pl.BlockSpec((2 * CB, CHUNK, LANES), lambda g: (0, 0, 0)),
-            pl.BlockSpec((2 * F, LAGS), lambda g: (0, 0)),
-        ],
+        in_specs=[pl.BlockSpec(memory_space=pltpu.VMEM)] * 2,
         out_specs=pl.BlockSpec((GROUP, CB, LAGS), lambda g: (g, 0, 0)),
         scratch_shapes=[
             pltpu.VMEM((2 * CB * CHUNK, LANES), F32),
             pltpu.VMEM((NWIN, CB, 2 * F), F32),
-            pltpu.VMEM((NWIN, CB, 2 * F), F32),
+            pltpu.VMEM((NWIN, CB, 2 * F), BF16),
             pltpu.VMEM((GROUP * CB, 2 * F), BF16),
         ],
         compiler_params=pltpu.CompilerParams(vmem_limit_bytes=32 * 2**20),

time: 73.5 us -> 67.6 us (0.920)
  local copies, waits for them, and re-layouts: 4.88 us -> 0.02 us
  Pallas kernels: 21.4 us -> 20.1 us
    unnamed x16 -> x8, local copies, waits for them, and re-layouts: 4.88 us -> 0.02 us
    pallas_call x1, Pallas kernels: 12.8 us -> 10.6 us  [pair_lags(): pl.pallas_call(lags_kernel, grid=(CB // GROUP,), out_shape=jax.ShapeDtype...]
    pallas_call x1, Pallas kernels: 4.98 us -> 6.24 us  [project(): pl.pallas_call(functools.partial(project_kernel, parts), out_shape=jax.Sh...]
where the time goes in v2:
time: 67.6 us; the launch traced here: 67.3 us
  blocking collectives  47.2 us (70%)
  Pallas kernels  20.1 us (30%)
    all_to_all x1, blocking collectives, per_device(): received = lax.all_to_all(coefs, 'chan', 0, 0, tiled=True)  24.7 us
    all_to_all x1, blocking collectives, per_device(): gathered = lax.all_to_all(chosen, ('tm', 'chan'), 0, 0, tiled=True)  22.4 us
    pallas_call x1, Pallas kernels, pair_lags(): pl.pallas_call(lags_kernel, grid=(CB // GROUP,), out_shape=jax.ShapeDtype...  10.6 us
    pallas_call x1, Pallas kernels, project(): pl.pallas_call(functools.partial(project_kernel, parts), out_shape=jax.Sh...  6.24 us
    pallas_call x1, Pallas kernels, whiten(): pl.pallas_call(whiten_kernel, out_shape=jax.ShapeDtypeStruct((2 * NB, CHU...  3.3 us

profile of v2, /device:TPU:1, one launch (start us, length us, event | category | flops | bytes accessed | tf_op | source)
XLA Modules:
  0.0 67.3 jit_solution(9006631063301119932)
XLA Ops:
  0.0 0.0 copy-start
  0.0 0.0 copy-start.2
  0.0 0.0 copy-start.1
  0.0 0.0 copy-start.3
  0.0 6.2 %project.1 = bf16[64,40,128]{2,1,0:T(8,128)(2,1)} custom-call(s32[2,1,2]{2,1,0:T(1,128)} %pairs_hbm.1, s32[64]{0:T(128)} %live_hbm.1, f32[24,250]{1,0:T(8,128)} %constant.10.clone.basis_ref, bf16[3,250,4096]{2,1,0:T(8,128)(2,1)} %x_hbm.1), custom_call_target="tpu_custom_call" | custom-call | flops 400000000 | bytes 7000000 | tf_op jit(solution)/shard_map/project/pallas_call | solution.py:153
  6.3 24.7 %all_to_all.10.r_ref = bf16[64,40,128]{2,1,0:T(8,128)(2,1)S(1)} all-to-all(bf16[64,40,128]{2,1,0:T(8,128)(2,1)} %project.1), channel_id=1, replica_groups=mesh['tm'=2,'chan'=64] {'chan'}, dimensions={0} | all-to-all | bytes 1310720 | tf_op jit(solution)/shard_map/channels_exchange/all_to_all | solution.py:327
  31.0 0.0 copy-done
  31.0 0.0 copy-done.2
  31.0 0.0 copy-done.1
  31.0 3.3 %whiten.1 = bf16[128,24,128]{2,1,0:T(8,128)(2,1)S(1)} custom-call(bf16[64,40,128]{2,1,0:T(8,128)(2,1)S(1)} %all_to_all.10.r_ref, bf16[640,1536]{1,0:T(8,128)(2,1)S(1)} %copy-done, bf16[256,320]{1,0:T(8,128)(2,1)S(1)} %copy-done.1, f32[1,512]{1,0:T(1,128)S(1)} %copy-done.2), custom_call_target="tpu_custom_call" | custom-call | flops 600000000 | bytes 4000000 | tf_op jit(solution)/shard_map/whiten/pallas_call | solution.py:231
  34.3 22.4 %all_to_all.11.g_ref = bf16[128,24,128]{2,1,0:T(8,128)(2,1)S(1)} all-to-all(bf16[128,24,128]{2,1,0:T(8,128)(2,1)S(1)} %whiten.1), channel_id=1, replica_groups=mesh['tm'=2,'chan'=64] {'tm','chan'}, dimensions={0} | all-to-all | bytes 1572864 | tf_op jit(solution)/shard_map/pairs_exchange/all_to_all | solution.py:330
  56.8 0.0 copy-done.3
  56.8 10.6 %pair_lags.1 = bf16[64,64,1024]{2,1,0:T(8,128)(2,1)} custom-call(bf16[128,24,128]{2,1,0:T(8,128)(2,1)S(1)} %all_to_all.11.g_ref, bf16[512,1024]{1,0:T(8,128)(2,1)S(1)} %copy-done.3), custom_call_target="tpu_custom_call" | custom-call | flops 4400000000 | bytes 12000000 | tf_op jit(solution)/shard_map/pair_lags/pallas_call | solution.py:298
Async XLA Ops:
  0.0 31.0 %copy-start = (bf16[640,1536]{1,0:T(8,128)(2,1)S(1)}, bf16[640,1536]{1,0:T(8,128)(2,1)}, u32[]{:S(2)}) copy-start(bf16[640,1536]{1,0:T(8,128)(2,1)} %constant.13.clone.table_ref) | copy-start | bytes 5898244
  0.0 31.0 %copy-start.2 = (f32[1,512]{1,0:T(1,128)S(1)}, f32[1,512]{1,0:T(1,128)}, u32[]{:S(2)}) copy-start(f32[1,512]{1,0:T(1,128)} %constant.12.clone.taper_ref) | copy-start | bytes 6148
  0.0 31.0 %copy-start.1 = (bf16[256,320]{1,0:T(8,128)(2,1)S(1)}, bf16[256,320]{1,0:T(8,128)(2,1)}, u32[]{:S(2)}) copy-start(bf16[256,320]{1,0:T(8,128)(2,1)} %constant.11.clone.ones_ref) | copy-start | bytes 491524
  0.0 56.8 %copy-start.3 = (bf16[512,1024]{1,0:T(8,128)(2,1)S(1)}, bf16[512,1024]{1,0:T(8,128)(2,1)}, u32[]{:S(2)}) copy-start(bf16[512,1024]{1,0:T(8,128)(2,1)} %constant.14.clone.back_ref) | copy-start | bytes 3145732

commit v3 on v2

--- a/solution.py
+++ b/solution.py
@@ -96,14 +96,18 @@
 
     def exchange(groups, bits, base):
         for bit in bits:
-            stride, shift = 1 << (bit - base), 1 << bit
+            stride = 1 << (bit - base)
             for v in range(len(groups[0])):
                 if v & stride:
                     continue
                 for z in groups:
                     x0, x1 = z[v], z[v | stride]
-                    z[v] = jnp.where(masks[bit], pltpu.roll(x1, shift, 1), x0)
-                    z[v | stride] = jnp.where(masks[bit], x1, pltpu.roll(x0, LANES - shift, 1))
+                    if bit:
+                        z[v] = jnp.where(masks[bit], x1, x0)
+                        z[v | stride] = jnp.where(masks[bit], x0, x1)
+                    else:
+                        z[v] = jnp.where(masks[0], pltpu.roll(x1, 1, 1), x0)
+                        z[v | stride] = jnp.where(masks[0], x1, pltpu.roll(x0, LANES - 1, 1))
 
     count = 2 * per
     local = count.bit_length() - 1
@@ -128,6 +132,7 @@
     for copy in small:
         copy.wait()
     lane = lax.broadcasted_iota(jnp.int32, (8, LANES), 1)
+    even = block & (NB - 2)
     extra = jnp.zeros((8, LANES), F32)
     for s in range(2):
         for side in range(2):
@@ -144,7 +149,7 @@
                     if k < 2:
                         o_ref[slab, 16 * k : 16 * k + 16] = value
                     else:
-                        added = jnp.where(lane == 9, live_ref[slab].astype(F32), extra)
+                        added = jnp.where(lane == 9, live_ref[slab ^ even].astype(F32), extra)
                         o_ref[slab, 32:40] = (value[:8].astype(F32) + added).astype(BF16)
 
 
@@ -173,20 +178,23 @@
     )(block_pairs, live_mask, basis, strain)
 
 
-def slot(index):
-    return ((index & 1) << 5) | (index >> 1)
+def slot(index, device):
+    return ((index & 1) << 5) | ((index ^ device) >> 1)
 
 
 def whiten_kernel(r_ref, table_ref, ones_ref, taper_ref, o_ref, extra_ref, index_ref, small_ref, spec_ref, rows_ref, sem):
+    me = lax.axis_index("chan")
     received = r_ref[...].astype(F32)
     unit = [received[:, 8 * u : 8 * u + 8].reshape(8 * NB, LANES) for u in range(UNITS)]
     extra_ref[...] = unit[4]
-    index_ref[...] = extra_ref[pl.ds(0, NB, stride=8), :].astype(jnp.int32)
+    extra = extra_ref[pl.ds(0, NB, stride=8), :]
+    index_ref[...] = slot(extra.astype(jnp.int32) & (NB - 1), me) * 16
     copy = pltpu.make_async_copy(index_ref, small_ref, sem)
     copy.start()
-    even = extra_ref[pl.ds(0, NB // 2, stride=16), :]
-    odd = extra_ref[pl.ds(8, NB // 2, stride=16), :]
-    live = jnp.concatenate([even, odd], 0)[:, 9:10]
+    place = lax.broadcasted_iota(jnp.int32, (NB, NB), 0)
+    wanted = slot(lax.broadcasted_iota(jnp.int32, (NB, NB), 1), me)
+    order = jnp.where(place == wanted, 1.0, 0.0).astype(BF16)
+    live = jnp.dot(order, extra.astype(BF16), preferred_element_type=F32)[:, 9:10]
     left = jnp.concatenate(unit[:3], 0)
     right = jnp.concatenate([unit[3], pltpu.roll(unit[3], LANES - 1, 1), unit[4]], 0)
     operand = jnp.concatenate([left, right], 1).astype(BF16)
@@ -196,7 +204,7 @@
     ones = ones_ref[...]
     total = jnp.zeros((F, 2 * LANES), F32)
     rest = magnitude
-    for _ in range(3):
+    for _ in range(2):
         piece = rest.astype(BF16)
         rest = rest - piece.astype(F32)
         total = total + jnp.dot(ones, piece, preferred_element_type=F32)
@@ -219,10 +227,10 @@
     @pl.loop(0, NB, unroll=8)
     def _(device):
         for s in range(2):
-            first = slot(small_ref[device, 1 + 4 * s])
-            second = slot(small_ref[device, 3 + 4 * s])
-            a = rows_ref[pl.ds(pl.multiple_of(first * 16, 16), 16), :]
-            b = rows_ref[pl.ds(pl.multiple_of(second * 16, 16), 16), :]
+            first = pl.multiple_of(small_ref[device, 1 + 4 * s], 16)
+            second = pl.multiple_of(small_ref[device, 3 + 4 * s], 16)
+            a = rows_ref[pl.ds(first, 16), :]
+            b = rows_ref[pl.ds(second, 16), :]
             chunk = jnp.concatenate([a[:8], jnp.where(low, a[8:], b[8:]), b[:8]], 0)
             o_ref[s * NB + device] = chunk.astype(BF16)
 
@@ -247,70 +255,114 @@
     )(received, table, ones, taper)
 
 
-GROUP = 16
-
-
-def lags_kernel(g_ref, back_ref, o_ref, flat_ref, a_ref, b_ref, cross_ref):
+GROUP = 8
+PIECES = 4
+JOBS = (2, 4, 4, 4)
+
+
+def lags_kernel(pairs_ref, g_ref, back_ref, o_ref, flat_ref, a_ref, b_ref, cross0_ref, cross1_ref):
     step = pl.program_id(0)
+    last = pl.num_programs(0) - 1
+
+    def spread(value):
+        return jnp.broadcast_to(value, (16, LANES)).astype(BF16)
+
+    def total(terms):
+        return ((terms[0] + terms[1]) + (terms[2] + terms[3])) + (terms[4] + terms[5])
+
+    def cross(channel, k, tile, cross_ref):
+        ar, ai = [], []
+        for win in range(NWIN):
+            at = (win // WIN_DEV) * CB + channel
+            row = (win % WIN_DEV) * 4 + tile
+            ar.append(spread(a_ref[at, row : row + 1, :]))
+            ai.append(spread(a_ref[at, row + 2 : row + 3, :]))
+        for start in range(0, CB, 16):
+            real, imag = [], []
+            for win in range(NWIN):
+                br = b_ref[win * 4 + tile, start : start + 16]
+                bi = b_ref[win * 4 + tile + 2, start : start + 16]
+                real.append(ar[win] * br + ai[win] * bi)
+                imag.append(ai[win] * br - ar[win] * bi)
+            rows = slice(k * CB + start, k * CB + start + 16)
+            cross_ref[rows, tile * LANES : (tile + 1) * LANES] = total(real)
+            cross_ref[rows, F + tile * LANES : F + (tile + 1) * LANES] = total(imag)
+
+    def both(ready_ref, next_ref):
+        jobs = [] if next_ref is None else [(k, tile) for k in range(GROUP) for tile in range(F // LANES)]
+
+        def run(chosen):
+            for k, tile in chosen:
+                cross(step * GROUP + k, k, tile, next_ref)
+
+        if ready_ref is None:
+            run(jobs)
+            return
+        width = LAGS // PIECES
+        done = 0
+        for piece in range(PIECES):
+            run(jobs[done : done + JOBS[piece]])
+            done += JOBS[piece]
+            cols = slice(piece * width, (piece + 1) * width)
+            lags = jnp.dot(ready_ref[...], back_ref[:, cols], preferred_element_type=F32)
+            o_ref[:, :, cols] = lags.astype(BF16).reshape(GROUP, CB, width)
+        run(jobs[done:])
 
     @pl.when(step == 0)
     def _():
-        flat_ref[...] = g_ref[...].astype(F32).reshape(2 * CB * CHUNK, LANES)
+        mine = lax.axis_index("tm")
+        first = pairs_ref[mine, 0, 0] & (NB - 2)
+        second = pairs_ref[mine, 0, 1] & (NB - 2)
+
+        @pl.loop(0, CB, unroll=4)
+        def _(source):
+            for group in range(2):
+                value = g_ref[group * CB + source].astype(F32)
+                a_ref[group * CB + (source ^ first)] = value
+                start = (group * CB + (source ^ second)) * CHUNK
+                flat_ref[pl.ds(pl.multiple_of(start, 8), CHUNK), :] = value
+
         for group in range(2):
-            for win in range(WIN_DEV):
-                for tile in range(2 * F // LANES):
-                    cols = slice(tile * LANES, (tile + 1) * LANES)
-                    at = win * 4 + tile
-                    places = (at, 12 + tile if win == 2 else 16 + at)
-                    for ref, place in zip((a_ref, b_ref), places):
-                        start = group * CB * CHUNK + place
-                        value = flat_ref[pl.ds(start, CB, stride=CHUNK), :]
-                        ref[group * WIN_DEV + win, :, cols] = value.astype(ref.dtype)
-
-    rows = pl.ds(pl.multiple_of(step * GROUP, GROUP), GROUP)
-
-    def spread(value):
-        value = jnp.broadcast_to(value, (16, LANES)).astype(BF16)
-        return jnp.concatenate([value] * (CB // 16), 0)
-
-    def total(terms):
-        return ((terms[0] + terms[1]) + (terms[2] + terms[3])) + (terms[4] + terms[5])
-
-    for k in range(GROUP):
-        for tile in range(F // LANES):
-            re = slice(tile * LANES, (tile + 1) * LANES)
-            im = slice(F + tile * LANES, F + (tile + 1) * LANES)
-            real, imag = [], []
-            for win in range(NWIN):
-                ar = spread(a_ref[win, rows, re][k : k + 1])
-                ai = spread(a_ref[win, rows, im][k : k + 1])
-                br = b_ref[win, :, re]
-                bi = b_ref[win, :, im]
-                real.append(ar * br + ai * bi)
-                imag.append(ai * br - ar * bi)
-            cross_ref[k * CB : (k + 1) * CB, re] = total(real)
-            cross_ref[k * CB : (k + 1) * CB, im] = total(imag)
-    lags = jnp.dot(cross_ref[...], back_ref[...], preferred_element_type=F32)
-    o_ref[...] = lags.astype(BF16).reshape(GROUP, CB, LAGS)
-
-
-def pair_lags(gathered, back):
+            for row in range(12):
+                start = group * CB * CHUNK + (16 + row if row < 8 else 4 + row)
+                b_ref[group * 12 + row] = flat_ref[pl.ds(start, CB, stride=CHUNK), :].astype(BF16)
+        both(None, cross0_ref)
+
+    @pl.when((step > 0) & (step < last) & (step % 2 == 1))
+    def _():
+        both(cross0_ref, cross1_ref)
+
+    @pl.when((step > 0) & (step < last) & (step % 2 == 0))
+    def _():
+        both(cross1_ref, cross0_ref)
+
+    @pl.when(step == last)
+    def _():
+        both(cross1_ref, None)
+
+
+def pair_lags(block_pairs, gathered, back):
     return pl.pallas_call(
         lags_kernel,
-        grid=(CB // GROUP,),
+        grid=(CB // GROUP + 1,),
         out_shape=jax.ShapeDtypeStruct((CB, CB, LAGS), BF16),
-        in_specs=[pl.BlockSpec(memory_space=pltpu.VMEM)] * 2,
-        out_specs=pl.BlockSpec((GROUP, CB, LAGS), lambda g: (g, 0, 0)),
+        in_specs=[
+            pl.BlockSpec(memory_space=pltpu.SMEM),
+            pl.BlockSpec(memory_space=pltpu.VMEM),
+            pl.BlockSpec(memory_space=pltpu.VMEM),
+        ],
+        out_specs=pl.BlockSpec((GROUP, CB, LAGS), lambda g: (jnp.maximum(g - 1, 0), 0, 0)),
         scratch_shapes=[
             pltpu.VMEM((2 * CB * CHUNK, LANES), F32),
-            pltpu.VMEM((NWIN, CB, 2 * F), F32),
-            pltpu.VMEM((NWIN, CB, 2 * F), BF16),
+            pltpu.VMEM((2 * CB, CHUNK, LANES), F32),
+            pltpu.VMEM((NWIN * 4, CB, LANES), BF16),
+            pltpu.VMEM((GROUP * CB, 2 * F), BF16),
             pltpu.VMEM((GROUP * CB, 2 * F), BF16),
         ],
         compiler_params=pltpu.CompilerParams(vmem_limit_bytes=32 * 2**20),
         cost_estimate=pl.CostEstimate(flops=4_400_000_000, bytes_accessed=12_000_000, transcendentals=0),
         name="pair_lags",
-    )(gathered, back)
+    )(block_pairs, gathered, back)
 
 
 def solution(mesh):
@@ -328,7 +380,7 @@
         chosen = whiten(received, jnp.asarray(table_np), ones, taper)
         with jax.named_scope("pairs_exchange"):
             gathered = lax.all_to_all(chosen, ("tm", "chan"), 0, 0, tiled=True)
-        return pair_lags(gathered, jnp.asarray(back_np)).reshape(1, 1, CB, CB, LAGS)
+        return pair_lags(block_pairs, gathered, jnp.asarray(back_np)).reshape(1, 1, CB, CB, LAGS)
 
     in_specs = (P("tm", "chan", None), P("chan"), P(None, "chan", None))
     out_specs = P("tm", "chan", None, None, None)

time: 67.6 us -> 65.7 us (0.972)
  Pallas kernels: 20.1 us -> 18.2 us
    pallas_call x1, Pallas kernels: 3.3 us -> 1.9 us  [whiten(): pl.pallas_call(whiten_kernel, out_shape=jax.ShapeDtypeStruct((2 * NB, CHU...]
where the time goes in v3:
time: 65.7 us; the launch traced here: 65.5 us
  blocking collectives  47.2 us (72%)
  Pallas kernels  18.2 us (28%)
    all_to_all x1, blocking collectives, per_device(): received = lax.all_to_all(coefs, 'chan', 0, 0, tiled=True)  24.7 us
    all_to_all x1, blocking collectives, per_device(): gathered = lax.all_to_all(chosen, ('tm', 'chan'), 0, 0, tiled=True)  22.4 us
    pallas_call x1, Pallas kernels, pair_lags(): pl.pallas_call(lags_kernel, grid=(CB // GROUP + 1,), out_shape=jax.ShapeD...  10.7 us
    pallas_call x1, Pallas kernels, project(): pl.pallas_call(functools.partial(project_kernel, parts), out_shape=jax.Sh...  5.58 us
    pallas_call x1, Pallas kernels, whiten(): pl.pallas_call(whiten_kernel, out_shape=jax.ShapeDtypeStruct((2 * NB, CHU...  1.9 us

profile of v3, /device:TPU:1, one launch (start us, length us, event | category | flops | bytes accessed | tf_op | source)
XLA Modules:
  0.0 65.5 jit_solution(5802483695811299883)
XLA Ops:
  0.0 0.0 copy-start
  0.0 0.0 copy-start.2
  0.0 0.0 copy-start.1
  0.0 0.0 copy-start.4
  0.0 0.0 copy-start.3
  0.0 5.6 %project.1 = bf16[64,40,128]{2,1,0:T(8,128)(2,1)} custom-call(s32[2,1,2]{2,1,0:T(1,128)} %pairs_ref.1, s32[64]{0:T(128)} %live_hbm.1, f32[24,250]{1,0:T(8,128)} %constant.10.clone.basis_ref, bf16[3,250,4096]{2,1,0:T(8,128)(2,1)} %x_hbm.1), custom_call_target="tpu_custom_call" | custom-call | flops 400000000 | bytes 7000000 | tf_op jit(solution)/shard_map/project/pallas_call | solution.py:158
  5.6 24.7 %all_to_all.10.r_ref = bf16[64,40,128]{2,1,0:T(8,128)(2,1)S(1)} all-to-all(bf16[64,40,128]{2,1,0:T(8,128)(2,1)} %project.1), channel_id=1, replica_groups=mesh['tm'=2,'chan'=64] {'chan'}, dimensions={0} | all-to-all | bytes 1310720 | tf_op jit(solution)/shard_map/channels_exchange/all_to_all | solution.py:379
  30.4 0.0 copy-done
  30.4 0.0 copy-done.2
  30.4 0.0 copy-done.1
  30.4 1.9 %whiten.1 = bf16[128,24,128]{2,1,0:T(8,128)(2,1)S(1)} custom-call(bf16[64,40,128]{2,1,0:T(8,128)(2,1)S(1)} %all_to_all.10.r_ref, bf16[640,1536]{1,0:T(8,128)(2,1)S(1)} %copy-done, bf16[256,320]{1,0:T(8,128)(2,1)S(1)} %copy-done.1, f32[1,512]{1,0:T(1,128)S(1)} %copy-done.2), custom_call_target="tpu_custom_call" | custom-call | flops 600000000 | bytes 4000000 | tf_op jit(solution)/shard_map/whiten/pallas_call | solution.py:239
  32.3 22.4 %all_to_all.11.g_ref = bf16[128,24,128]{2,1,0:T(8,128)(2,1)S(1)} all-to-all(bf16[128,24,128]{2,1,0:T(8,128)(2,1)S(1)} %whiten.1), channel_id=1, replica_groups=mesh['tm'=2,'chan'=64] {'tm','chan'}, dimensions={0} | all-to-all | bytes 1572864 | tf_op jit(solution)/shard_map/pairs_exchange/all_to_all | solution.py:382
  54.7 0.0 copy-done.4
  54.7 0.0 copy-done.3
  54.7 10.7 %pair_lags.1 = bf16[64,64,1024]{2,1,0:T(8,128)(2,1)} custom-call(s32[2,1,2]{2,1,0:T(1,128)S(1)} %copy-done.3, bf16[128,24,128]{2,1,0:T(8,128)(2,1)S(1)} %all_to_all.11.g_ref, bf16[512,1024]{1,0:T(8,128)(2,1)S(1)} %copy-done.4), custom_call_target="tpu_custom_call" | custom-call | flops 4400000000 | bytes 12000000 | tf_op jit(solution)/shard_map/pair_lags/pallas_call | solution.py:345
Async XLA Ops:
  0.0 30.4 %copy-start = (bf16[640,1536]{1,0:T(8,128)(2,1)S(1)}, bf16[640,1536]{1,0:T(8,128)(2,1)}, u32[]{:S(2)}) copy-start(bf16[640,1536]{1,0:T(8,128)(2,1)} %constant.13.clone.table_ref) | copy-start | bytes 5898244
  0.0 30.4 %copy-start.2 = (f32[1,512]{1,0:T(1,128)S(1)}, f32[1,512]{1,0:T(1,128)}, u32[]{:S(2)}) copy-start(f32[1,512]{1,0:T(1,128)} %constant.12.clone.taper_ref) | copy-start | bytes 6148
  0.0 30.4 %copy-start.1 = (bf16[256,320]{1,0:T(8,128)(2,1)S(1)}, bf16[256,320]{1,0:T(8,128)(2,1)}, u32[]{:S(2)}) copy-start(bf16[256,320]{1,0:T(8,128)(2,1)} %constant.11.clone.ones_ref) | copy-start | bytes 491524
  0.0 54.7 %copy-start.4 = (bf16[512,1024]{1,0:T(8,128)(2,1)S(1)}, bf16[512,1024]{1,0:T(8,128)(2,1)}, u32[]{:S(2)}) copy-start(bf16[512,1024]{1,0:T(8,128)(2,1)} %constant.14.clone.back_ref) | copy-start | bytes 3145732
  0.0 54.7 %copy-start.3 = (s32[2,1,2]{2,1,0:T(1,128)S(1)}, s32[2,1,2]{2,1,0:T(1,128)}, u32[]{:S(2)}) copy-start(s32[2,1,2]{2,1,0:T(1,128)} %pairs_ref.1) | copy-start | bytes 52

commit v4 on v3

--- a/solution.py
+++ b/solution.py
@@ -21,6 +21,7 @@
 LAGS = 1024
 SAMPLES = W // NB
 RANK = 24
+LAG_RANK = 64
 UNITS = 5
 ROWS = 8 * UNITS
 CHUNK = 24
@@ -31,15 +32,23 @@
 BF16 = jnp.bfloat16
 
 
+def prolate(size, band, count):
+    places = np.arange(size)
+    main = ((size - 1 - 2 * places) / 2.0) ** 2 * np.cos(2 * np.pi * band / W)
+    side = places[1:] * (size - places[1:]) / 2.0
+    _, vectors = np.linalg.eigh(np.diag(main) + np.diag(side, 1) + np.diag(side, -1))
+    basis = vectors[:, ::-1][:, :count]
+    mid = size // 2
+    centre = np.where(np.arange(count) % 2 == 0, basis[mid] + basis[mid - 1], basis[mid] - basis[mid - 1])
+    return basis * np.sign(centre)[None, :]
+
+
 def time_basis():
-    places = np.arange(SAMPLES)
-    main = ((SAMPLES - 1 - 2 * places) / 2.0) ** 2 * np.cos(2 * np.pi * (K0 - HALF + WIDTH) / W)
-    side = places[1:] * (SAMPLES - places[1:]) / 2.0
-    _, vectors = np.linalg.eigh(np.diag(main) + np.diag(side, 1) + np.diag(side, -1))
-    basis = vectors[:, ::-1][:, :RANK]
-    mid = SAMPLES // 2
-    centre = np.where(np.arange(RANK) % 2 == 0, basis[mid] + basis[mid - 1], basis[mid] - basis[mid - 1])
-    return basis * np.sign(centre)[None, :]
+    return prolate(SAMPLES, K0 - HALF + WIDTH, RANK)
+
+
+def lag_basis():
+    return prolate(LAGS, K0 + F, LAG_RANK)
 
 
 def block_tables(basis):
@@ -154,7 +163,7 @@
 
 
 def project(strain, live_mask, block_pairs, basis):
-    parts = 2
+    parts = 4
     return pl.pallas_call(
         functools.partial(project_kernel, parts),
         out_shape=jax.ShapeDtypeStruct((CB, ROWS, LANES), BF16),
@@ -260,7 +269,7 @@
 JOBS = (2, 4, 4, 4)
 
 
-def lags_kernel(pairs_ref, g_ref, back_ref, o_ref, flat_ref, a_ref, b_ref, cross0_ref, cross1_ref):
+def lags_kernel(pairs_ref, g_ref, reduce_ref, back_ref, o_ref, flat_ref, a_ref, b_ref, cross0_ref, cross1_ref, low0_ref, low1_ref):
     step = pl.program_id(0)
     last = pl.num_programs(0) - 1
 
@@ -288,23 +297,22 @@
             cross_ref[rows, tile * LANES : (tile + 1) * LANES] = total(real)
             cross_ref[rows, F + tile * LANES : F + (tile + 1) * LANES] = total(imag)
 
-    def both(ready_ref, next_ref):
+    def stage(next_ref, ready_ref, low_ref, done_ref):
         jobs = [] if next_ref is None else [(k, tile) for k in range(GROUP) for tile in range(F // LANES)]
 
         def run(chosen):
             for k, tile in chosen:
                 cross(step * GROUP + k, k, tile, next_ref)
 
-        if ready_ref is None:
-            run(jobs)
-            return
+        if ready_ref is not None:
+            low_ref[...] = jnp.dot(ready_ref[...], reduce_ref[...], preferred_element_type=F32).astype(BF16)
         width = LAGS // PIECES
         done = 0
-        for piece in range(PIECES):
+        for piece in range(PIECES if done_ref is not None else 0):
             run(jobs[done : done + JOBS[piece]])
             done += JOBS[piece]
             cols = slice(piece * width, (piece + 1) * width)
-            lags = jnp.dot(ready_ref[...], back_ref[:, cols], preferred_element_type=F32)
+            lags = jnp.dot(done_ref[...], back_ref[:, cols], preferred_element_type=F32)
             o_ref[:, :, cols] = lags.astype(BF16).reshape(GROUP, CB, width)
         run(jobs[done:])
 
@@ -326,49 +334,62 @@
             for row in range(12):
                 start = group * CB * CHUNK + (16 + row if row < 8 else 4 + row)
                 b_ref[group * 12 + row] = flat_ref[pl.ds(start, CB, stride=CHUNK), :].astype(BF16)
-        both(None, cross0_ref)
-
-    @pl.when((step > 0) & (step < last) & (step % 2 == 1))
-    def _():
-        both(cross0_ref, cross1_ref)
-
-    @pl.when((step > 0) & (step < last) & (step % 2 == 0))
-    def _():
-        both(cross1_ref, cross0_ref)
+        stage(cross0_ref, None, None, None)
+
+    @pl.when(step == 1)
+    def _():
+        stage(cross1_ref, cross0_ref, low0_ref, None)
+
+    @pl.when((step > 1) & (step < last - 1) & (step % 2 == 0))
+    def _():
+        stage(cross0_ref, cross1_ref, low1_ref, low0_ref)
+
+    @pl.when((step > 1) & (step < last - 1) & (step % 2 == 1))
+    def _():
+        stage(cross1_ref, cross0_ref, low0_ref, low1_ref)
+
+    @pl.when(step == last - 1)
+    def _():
+        stage(None, cross1_ref, low1_ref, low0_ref)
 
     @pl.when(step == last)
     def _():
-        both(cross1_ref, None)
-
-
-def pair_lags(block_pairs, gathered, back):
+        stage(None, None, None, low1_ref)
+
+
+def pair_lags(block_pairs, gathered, reduce, back):
     return pl.pallas_call(
         lags_kernel,
-        grid=(CB // GROUP + 1,),
+        grid=(CB // GROUP + 2,),
         out_shape=jax.ShapeDtypeStruct((CB, CB, LAGS), BF16),
         in_specs=[
             pl.BlockSpec(memory_space=pltpu.SMEM),
             pl.BlockSpec(memory_space=pltpu.VMEM),
             pl.BlockSpec(memory_space=pltpu.VMEM),
+            pl.BlockSpec(memory_space=pltpu.VMEM),
         ],
-        out_specs=pl.BlockSpec((GROUP, CB, LAGS), lambda g: (jnp.maximum(g - 1, 0), 0, 0)),
+        out_specs=pl.BlockSpec((GROUP, CB, LAGS), lambda g: (jnp.maximum(g - 2, 0), 0, 0)),
         scratch_shapes=[
             pltpu.VMEM((2 * CB * CHUNK, LANES), F32),
             pltpu.VMEM((2 * CB, CHUNK, LANES), F32),
             pltpu.VMEM((NWIN * 4, CB, LANES), BF16),
             pltpu.VMEM((GROUP * CB, 2 * F), BF16),
             pltpu.VMEM((GROUP * CB, 2 * F), BF16),
+            pltpu.VMEM((GROUP * CB, LAG_RANK), BF16),
+            pltpu.VMEM((GROUP * CB, LAG_RANK), BF16),
         ],
         compiler_params=pltpu.CompilerParams(vmem_limit_bytes=32 * 2**20),
-        cost_estimate=pl.CostEstimate(flops=4_400_000_000, bytes_accessed=12_000_000, transcendentals=0),
+        cost_estimate=pl.CostEstimate(flops=900_000_000, bytes_accessed=12_000_000, transcendentals=0),
         name="pair_lags",
-    )(block_pairs, gathered, back)
+    )(block_pairs, gathered, reduce, back)
 
 
 def solution(mesh):
     basis_np = time_basis()
     table_np = block_tables(basis_np).astype(jnp.bfloat16)
-    back_np = lag_table().astype(jnp.bfloat16)
+    lag_np = lag_basis()
+    reduce_np = (lag_table() @ lag_np).astype(jnp.bfloat16)
+    back_np = lag_np.T.astype(jnp.bfloat16)
 
     def per_device(strain, live_mask, block_pairs):
         basis = jnp.asarray(basis_np.T.astype(np.float32))
@@ -380,7 +401,7 @@
         chosen = whiten(received, jnp.asarray(table_np), ones, taper)
         with jax.named_scope("pairs_exchange"):
             gathered = lax.all_to_all(chosen, ("tm", "chan"), 0, 0, tiled=True)
-        return pair_lags(block_pairs, gathered, jnp.asarray(back_np)).reshape(1, 1, CB, CB, LAGS)
+        return pair_lags(block_pairs, gathered, jnp.asarray(reduce_np), jnp.asarray(back_np)).reshape(1, 1, CB, CB, LAGS)
 
     in_specs = (P("tm", "chan", None), P("chan"), P(None, "chan", None))
     out_specs = P("tm", "chan", None, None, None)

time: 65.7 us -> 65 us (0.989)
  Pallas kernels: 18.2 us -> 17.5 us
where the time goes in v4:
time: 65 us; the launch traced here: 64.8 us
  blocking collectives  47.2 us (73%)
  Pallas kernels  17.5 us (27%)
    all_to_all x1, blocking collectives, per_device(): received = lax.all_to_all(coefs, 'chan', 0, 0, tiled=True)  24.7 us
    all_to_all x1, blocking collectives, per_device(): gathered = lax.all_to_all(chosen, ('tm', 'chan'), 0, 0, tiled=True)  22.4 us
    pallas_call x1, Pallas kernels, pair_lags(): pl.pallas_call(lags_kernel, grid=(CB // GROUP + 2,), out_shape=jax.ShapeD...  10.4 us
    pallas_call x1, Pallas kernels, project(): pl.pallas_call(functools.partial(project_kernel, parts), out_shape=jax.Sh...  5.26 us
    pallas_call x1, Pallas kernels, whiten(): pl.pallas_call(whiten_kernel, out_shape=jax.ShapeDtypeStruct((2 * NB, CHU...  1.9 us

profile of v4, /device:TPU:1, one launch (start us, length us, event | category | flops | bytes accessed | tf_op | source)
XLA Modules:
  0.0 64.8 jit_solution(16192869807595580092)
XLA Ops:
  0.0 0.0 copy-start
  0.0 0.0 copy-start.5
  0.0 0.0 copy-start.1
  0.0 0.0 copy-start.2
  0.0 0.0 copy-start.3
  0.0 0.0 copy-start.4
  0.0 5.3 %project.1 = bf16[64,40,128]{2,1,0:T(8,128)(2,1)} custom-call(s32[2,1,2]{2,1,0:T(1,128)} %pairs_ref.1, s32[64]{0:T(128)} %live_hbm.1, f32[24,250]{1,0:T(8,128)} %constant.12.clone.basis_ref, bf16[3,250,4096]{2,1,0:T(8,128)(2,1)} %x_hbm.1), custom_call_target="tpu_custom_call" | custom-call | flops 400000000 | bytes 7000000 | tf_op jit(solution)/shard_map/project/pallas_call | solution.py:167
  5.3 24.7 %all_to_all.10.r_ref = bf16[64,40,128]{2,1,0:T(8,128)(2,1)S(1)} all-to-all(bf16[64,40,128]{2,1,0:T(8,128)(2,1)} %project.1), channel_id=1, replica_groups=mesh['tm'=2,'chan'=64] {'chan'}, dimensions={0} | all-to-all | bytes 1310720 | tf_op jit(solution)/shard_map/channels_exchange/all_to_all | solution.py:400
  30.1 0.0 copy-done
  30.1 0.0 copy-done.5
  30.1 0.0 copy-done.1
  30.1 1.9 %whiten.1 = bf16[128,24,128]{2,1,0:T(8,128)(2,1)S(1)} custom-call(bf16[64,40,128]{2,1,0:T(8,128)(2,1)S(1)} %all_to_all.10.r_ref, bf16[640,1536]{1,0:T(8,128)(2,1)S(1)} %copy-done, bf16[256,320]{1,0:T(8,128)(2,1)S(1)} %copy-done.1, f32[1,512]{1,0:T(1,128)S(1)} %copy-done.5), custom_call_target="tpu_custom_call" | custom-call | flops 600000000 | bytes 4000000 | tf_op jit(solution)/shard_map/whiten/pallas_call | solution.py:248
  32.0 22.4 %all_to_all.11.g_ref = bf16[128,24,128]{2,1,0:T(8,128)(2,1)S(1)} all-to-all(bf16[128,24,128]{2,1,0:T(8,128)(2,1)S(1)} %whiten.1), channel_id=1, replica_groups=mesh['tm'=2,'chan'=64] {'tm','chan'}, dimensions={0} | all-to-all | bytes 1572864 | tf_op jit(solution)/shard_map/pairs_exchange/all_to_all | solution.py:403
  54.4 0.0 copy-done.2
  54.4 0.0 copy-done.3
  54.4 0.0 copy-done.4
  54.4 10.4 %pair_lags.1 = bf16[64,64,1024]{2,1,0:T(8,128)(2,1)} custom-call(s32[2,1,2]{2,1,0:T(1,128)S(1)} %copy-done.4, bf16[128,24,128]{2,1,0:T(8,128)(2,1)S(1)} %all_to_all.11.g_ref, bf16[512,64]{1,0:T(8,128)(2,1)S(1)} %copy-done.3, bf16[64,1024]{1,0:T(8,128)(2,1)S(1)} %copy-done.2), custom_call_target="tpu_custom_call" | custom-call | flops 900000000 | bytes 12000000 | tf_op jit(solution)/shard_map/pair_lags/pallas_call | solution.py:361
Async XLA Ops:
  0.0 30.1 %copy-start = (bf16[640,1536]{1,0:T(8,128)(2,1)S(1)}, bf16[640,1536]{1,0:T(8,128)(2,1)}, u32[]{:S(2)}) copy-start(bf16[640,1536]{1,0:T(8,128)(2,1)} %constant.15.clone.table_ref) | copy-start | bytes 5898244
  0.0 30.1 %copy-start.5 = (f32[1,512]{1,0:T(1,128)S(1)}, f32[1,512]{1,0:T(1,128)}, u32[]{:S(2)}) copy-start(f32[1,512]{1,0:T(1,128)} %constant.14.clone.taper_ref) | copy-start | bytes 6148
  0.0 30.1 %copy-start.1 = (bf16[256,320]{1,0:T(8,128)(2,1)S(1)}, bf16[256,320]{1,0:T(8,128)(2,1)}, u32[]{:S(2)}) copy-start(bf16[256,320]{1,0:T(8,128)(2,1)} %constant.13.clone.ones_ref) | copy-start | bytes 491524
  0.0 54.4 %copy-start.2 = (bf16[64,1024]{1,0:T(8,128)(2,1)S(1)}, bf16[64,1024]{1,0:T(8,128)(2,1)}, u32[]{:S(2)}) copy-start(bf16[64,1024]{1,0:T(8,128)(2,1)} %constant.17.clone.back_ref) | copy-start | bytes 393220
  0.0 54.4 %copy-start.3 = (bf16[512,64]{1,0:T(8,128)(2,1)S(1)}, bf16[512,64]{1,0:T(8,128)(2,1)}, u32[]{:S(2)}) copy-start(bf16[512,64]{1,0:T(8,128)(2,1)} %constant.16.clone.reduce_ref) | copy-start | bytes 196612
  0.0 54.4 %copy-start.4 = (s32[2,1,2]{2,1,0:T(1,128)S(1)}, s32[2,1,2]{2,1,0:T(1,128)}, u32[]{:S(2)}) copy-start(s32[2,1,2]{2,1,0:T(1,128)} %pairs_ref.1) | copy-start | bytes 52

commit v5 on v4

--- a/solution.py
+++ b/solution.py
@@ -319,8 +319,10 @@
     @pl.when(step == 0)
     def _():
         mine = lax.axis_index("tm")
-        first = pairs_ref[mine, 0, 0] & (NB - 2)
-        second = pairs_ref[mine, 0, 1] & (NB - 2)
+        pair = jnp.where(mine == 0, pairs_ref[0], pairs_ref[1]).astype(F32)
+        side = lax.broadcasted_iota(jnp.int32, pair.shape, 1)
+        first = jnp.sum(jnp.where(side == 0, pair, 0.0)).astype(jnp.int32) & (NB - 2)
+        second = jnp.sum(jnp.where(side == 1, pair, 0.0)).astype(jnp.int32) & (NB - 2)
 
         @pl.loop(0, CB, unroll=4)
         def _(source):
@@ -363,7 +365,7 @@
         grid=(CB // GROUP + 2,),
         out_shape=jax.ShapeDtypeStruct((CB, CB, LAGS), BF16),
         in_specs=[
-            pl.BlockSpec(memory_space=pltpu.SMEM),
+            pl.BlockSpec(memory_space=pltpu.VMEM),
             pl.BlockSpec(memory_space=pltpu.VMEM),
             pl.BlockSpec(memory_space=pltpu.VMEM),
             pl.BlockSpec(memory_space=pltpu.VMEM),

time: 65 us -> 64.5 us (level)
  no operation moved by 1% of the time
where the time goes in v5:
time: 64.5 us; the launch traced here: 64.3 us
  blocking collectives  47.2 us (73%)
  Pallas kernels  17 us (26%)
    all_to_all x1, blocking collectives, per_device(): received = lax.all_to_all(coefs, 'chan', 0, 0, tiled=True)  24.7 us
    all_to_all x1, blocking collectives, per_device(): gathered = lax.all_to_all(chosen, ('tm', 'chan'), 0, 0, tiled=True)  22.4 us
    pallas_call x1, Pallas kernels, pair_lags(): pl.pallas_call(lags_kernel, grid=(CB // GROUP + 2,), out_shape=jax.ShapeD...  9.86 us
    pallas_call x1, Pallas kernels, project(): pl.pallas_call(functools.partial(project_kernel, parts), out_shape=jax.Sh...  5.26 us
    pallas_call x1, Pallas kernels, whiten(): pl.pallas_call(whiten_kernel, out_shape=jax.ShapeDtypeStruct((2 * NB, CHU...  1.9 us

profile of v5, /device:TPU:1, one launch (start us, length us, event | category | flops | bytes accessed | tf_op | source)
XLA Modules:
  0.0 64.3 jit_solution(836752446834375673)
XLA Ops:
  0.0 0.0 copy-start
  0.0 0.0 copy-start.5
  0.0 0.0 copy-start.1
  0.0 0.0 copy-start.2
  0.0 0.0 copy-start.3
  0.0 0.0 copy-start.4
  0.0 5.3 %project.1 = bf16[64,40,128]{2,1,0:T(8,128)(2,1)} custom-call(s32[2,1,2]{2,1,0:T(1,128)} %pairs_ref.1, s32[64]{0:T(128)} %live_hbm.1, f32[24,250]{1,0:T(8,128)} %constant.12.clone.basis_ref, bf16[3,250,4096]{2,1,0:T(8,128)(2,1)} %x_hbm.1), custom_call_target="tpu_custom_call" | custom-call | flops 400000000 | bytes 7000000 | tf_op jit(solution)/shard_map/project/pallas_call | solution.py:167
  5.3 24.7 %all_to_all.10.r_ref = bf16[64,40,128]{2,1,0:T(8,128)(2,1)S(1)} all-to-all(bf16[64,40,128]{2,1,0:T(8,128)(2,1)} %project.1), channel_id=1, replica_groups=mesh['tm'=2,'chan'=64] {'chan'}, dimensions={0} | all-to-all | bytes 1310720 | tf_op jit(solution)/shard_map/channels_exchange/all_to_all | solution.py:402
  30.1 0.0 copy-done
  30.1 0.0 copy-done.5
  30.1 0.0 copy-done.1
  30.1 1.9 %whiten.1 = bf16[128,24,128]{2,1,0:T(8,128)(2,1)S(1)} custom-call(bf16[64,40,128]{2,1,0:T(8,128)(2,1)S(1)} %all_to_all.10.r_ref, bf16[640,1536]{1,0:T(8,128)(2,1)S(1)} %copy-done, bf16[256,320]{1,0:T(8,128)(2,1)S(1)} %copy-done.1, f32[1,512]{1,0:T(1,128)S(1)} %copy-done.5), custom_call_target="tpu_custom_call" | custom-call | flops 600000000 | bytes 4000000 | tf_op jit(solution)/shard_map/whiten/pallas_call | solution.py:248
  32.0 22.4 %all_to_all.11.g_ref = bf16[128,24,128]{2,1,0:T(8,128)(2,1)S(1)} all-to-all(bf16[128,24,128]{2,1,0:T(8,128)(2,1)S(1)} %whiten.1), channel_id=1, replica_groups=mesh['tm'=2,'chan'=64] {'tm','chan'}, dimensions={0} | all-to-all | bytes 1572864 | tf_op jit(solution)/shard_map/pairs_exchange/all_to_all | solution.py:405
  54.4 0.0 copy-done.2
  54.4 0.0 copy-done.3
  54.4 0.0 copy-done.4
  54.4 9.9 %pair_lags.1 = bf16[64,64,1024]{2,1,0:T(8,128)(2,1)} custom-call(s32[2,1,2]{2,1,0:T(1,128)S(1)} %copy-done.4, bf16[128,24,128]{2,1,0:T(8,128)(2,1)S(1)} %all_to_all.11.g_ref, bf16[512,64]{1,0:T(8,128)(2,1)S(1)} %copy-done.3, bf16[64,1024]{1,0:T(8,128)(2,1)S(1)} %copy-done.2), custom_call_target="tpu_custom_call" | custom-call | flops 900000000 | bytes 12000000 | tf_op jit(solution)/shard_map/pair_lags/pallas_call | solution.py:363
Async XLA Ops:
  0.0 30.1 %copy-start = (bf16[640,1536]{1,0:T(8,128)(2,1)S(1)}, bf16[640,1536]{1,0:T(8,128)(2,1)}, u32[]{:S(2)}) copy-start(bf16[640,1536]{1,0:T(8,128)(2,1)} %constant.15.clone.table_ref) | copy-start | bytes 5898244
  0.0 30.1 %copy-start.5 = (f32[1,512]{1,0:T(1,128)S(1)}, f32[1,512]{1,0:T(1,128)}, u32[]{:S(2)}) copy-start(f32[1,512]{1,0:T(1,128)} %constant.14.clone.taper_ref) | copy-start | bytes 6148
  0.0 30.1 %copy-start.1 = (bf16[256,320]{1,0:T(8,128)(2,1)S(1)}, bf16[256,320]{1,0:T(8,128)(2,1)}, u32[]{:S(2)}) copy-start(bf16[256,320]{1,0:T(8,128)(2,1)} %constant.13.clone.ones_ref) | copy-start | bytes 491524
  0.0 54.4 %copy-start.2 = (bf16[64,1024]{1,0:T(8,128)(2,1)S(1)}, bf16[64,1024]{1,0:T(8,128)(2,1)}, u32[]{:S(2)}) copy-start(bf16[64,1024]{1,0:T(8,128)(2,1)} %constant.17.clone.back_ref) | copy-start | bytes 393220
  0.0 54.4 %copy-start.3 = (bf16[512,64]{1,0:T(8,128)(2,1)S(1)}, bf16[512,64]{1,0:T(8,128)(2,1)}, u32[]{:S(2)}) copy-start(bf16[512,64]{1,0:T(8,128)(2,1)} %constant.16.clone.reduce_ref) | copy-start | bytes 196612
  0.0 54.4 %copy-start.4 = (s32[2,1,2]{2,1,0:T(1,128)S(1)}, s32[2,1,2]{2,1,0:T(1,128)}, u32[]{:S(2)}) copy-start(s32[2,1,2]{2,1,0:T(1,128)} %pairs_ref.1) | copy-start | bytes 52

commit v6 on v5

--- a/solution.py
+++ b/solution.py
@@ -269,7 +269,7 @@
 JOBS = (2, 4, 4, 4)
 
 
-def lags_kernel(pairs_ref, g_ref, reduce_ref, back_ref, o_ref, flat_ref, a_ref, b_ref, cross0_ref, cross1_ref, low0_ref, low1_ref):
+def lags_kernel(pairs_ref, g_ref, reduce_ref, back_ref, o_ref, flat_ref, b_ref, cross0_ref, cross1_ref, low0_ref, low1_ref, turn_ref):
     step = pl.program_id(0)
     last = pl.num_programs(0) - 1
 
@@ -282,10 +282,11 @@
     def cross(channel, k, tile, cross_ref):
         ar, ai = [], []
         for win in range(NWIN):
-            at = (win // WIN_DEV) * CB + channel
+            at = ((win // WIN_DEV) * CB + (channel ^ turn_ref[0])) * CHUNK
             row = (win % WIN_DEV) * 4 + tile
-            ar.append(spread(a_ref[at, row : row + 1, :]))
-            ai.append(spread(a_ref[at, row + 2 : row + 3, :]))
+            for rows, place in ((ar, row), (ai, row + 2)):
+                start = pl.multiple_of(at + place // 8 * 8, 8)
+                rows.append(spread(flat_ref[pl.ds(start, 8), :][place % 8 : place % 8 + 1]))
         for start in range(0, CB, 16):
             real, imag = [], []
             for win in range(NWIN):
@@ -323,12 +324,12 @@
         side = lax.broadcasted_iota(jnp.int32, pair.shape, 1)
         first = jnp.sum(jnp.where(side == 0, pair, 0.0)).astype(jnp.int32) & (NB - 2)
         second = jnp.sum(jnp.where(side == 1, pair, 0.0)).astype(jnp.int32) & (NB - 2)
+        turn_ref[0] = first ^ second
 
         @pl.loop(0, CB, unroll=4)
         def _(source):
             for group in range(2):
                 value = g_ref[group * CB + source].astype(F32)
-                a_ref[group * CB + (source ^ first)] = value
                 start = (group * CB + (source ^ second)) * CHUNK
                 flat_ref[pl.ds(pl.multiple_of(start, 8), CHUNK), :] = value
 
@@ -373,12 +374,12 @@
         out_specs=pl.BlockSpec((GROUP, CB, LAGS), lambda g: (jnp.maximum(g - 2, 0), 0, 0)),
         scratch_shapes=[
             pltpu.VMEM((2 * CB * CHUNK, LANES), F32),
-            pltpu.VMEM((2 * CB, CHUNK, LANES), F32),
             pltpu.VMEM((NWIN * 4, CB, LANES), BF16),
             pltpu.VMEM((GROUP * CB, 2 * F), BF16),
             pltpu.VMEM((GROUP * CB, 2 * F), BF16),
             pltpu.VMEM((GROUP * CB, LAG_RANK), BF16),
             pltpu.VMEM((GROUP * CB, LAG_RANK), BF16),
+            pltpu.SMEM((1,), jnp.int32),
         ],
         compiler_params=pltpu.CompilerParams(vmem_limit_bytes=32 * 2**20),
         cost_estimate=pl.CostEstimate(flops=900_000_000, bytes_accessed=12_000_000, transcendentals=0),

time: 64.5 us -> 64.4 us (level)
  no operation moved by 1% of the time
where the time goes in v6:
time: 64.4 us; the launch traced here: 64.2 us
  blocking collectives  47.2 us (73%)
  Pallas kernels  16.9 us (26%)
    all_to_all x1, blocking collectives, per_device(): received = lax.all_to_all(coefs, 'chan', 0, 0, tiled=True)  24.7 us
    all_to_all x1, blocking collectives, per_device(): gathered = lax.all_to_all(chosen, ('tm', 'chan'), 0, 0, tiled=True)  22.4 us
    pallas_call x1, Pallas kernels, pair_lags(): pl.pallas_call(lags_kernel, grid=(CB // GROUP + 2,), out_shape=jax.ShapeD...  9.78 us
    pallas_call x1, Pallas kernels, project(): pl.pallas_call(functools.partial(project_kernel, parts), out_shape=jax.Sh...  5.26 us
    pallas_call x1, Pallas kernels, whiten(): pl.pallas_call(whiten_kernel, out_shape=jax.ShapeDtypeStruct((2 * NB, CHU...  1.9 us

profile of v6, /device:TPU:1, one launch (start us, length us, event | category | flops | bytes accessed | tf_op | source)
XLA Modules:
  0.0 64.2 jit_solution(3531457422461997741)
XLA Ops:
  0.0 0.0 copy-start
  0.0 0.0 copy-start.5
  0.0 0.0 copy-start.1
  0.0 0.0 copy-start.2
  0.0 0.0 copy-start.3
  0.0 0.0 copy-start.4
  0.0 5.3 %project.1 = bf16[64,40,128]{2,1,0:T(8,128)(2,1)} custom-call(s32[2,1,2]{2,1,0:T(1,128)} %pairs_ref.1, s32[64]{0:T(128)} %live_hbm.1, f32[24,250]{1,0:T(8,128)} %constant.12.clone.basis_ref, bf16[3,250,4096]{2,1,0:T(8,128)(2,1)} %x_hbm.1), custom_call_target="tpu_custom_call" | custom-call | flops 400000000 | bytes 7000000 | tf_op jit(solution)/shard_map/project/pallas_call | solution.py:167
  5.3 24.7 %all_to_all.10.r_ref = bf16[64,40,128]{2,1,0:T(8,128)(2,1)S(1)} all-to-all(bf16[64,40,128]{2,1,0:T(8,128)(2,1)} %project.1), channel_id=1, replica_groups=mesh['tm'=2,'chan'=64] {'chan'}, dimensions={0} | all-to-all | bytes 1310720 | tf_op jit(solution)/shard_map/channels_exchange/all_to_all | solution.py:403
  30.1 0.0 copy-done
  30.1 0.0 copy-done.5
  30.1 0.0 copy-done.1
  30.1 1.9 %whiten.1 = bf16[128,24,128]{2,1,0:T(8,128)(2,1)S(1)} custom-call(bf16[64,40,128]{2,1,0:T(8,128)(2,1)S(1)} %all_to_all.10.r_ref, bf16[640,1536]{1,0:T(8,128)(2,1)S(1)} %copy-done, bf16[256,320]{1,0:T(8,128)(2,1)S(1)} %copy-done.1, f32[1,512]{1,0:T(1,128)S(1)} %copy-done.5), custom_call_target="tpu_custom_call" | custom-call | flops 600000000 | bytes 4000000 | tf_op jit(solution)/shard_map/whiten/pallas_call | solution.py:248
  32.0 22.4 %all_to_all.11.g_ref = bf16[128,24,128]{2,1,0:T(8,128)(2,1)S(1)} all-to-all(bf16[128,24,128]{2,1,0:T(8,128)(2,1)S(1)} %whiten.1), channel_id=1, replica_groups=mesh['tm'=2,'chan'=64] {'tm','chan'}, dimensions={0} | all-to-all | bytes 1572864 | tf_op jit(solution)/shard_map/pairs_exchange/all_to_all | solution.py:406
  54.4 0.0 copy-done.2
  54.4 0.0 copy-done.3
  54.4 0.0 copy-done.4
  54.4 9.8 %pair_lags.1 = bf16[64,64,1024]{2,1,0:T(8,128)(2,1)} custom-call(s32[2,1,2]{2,1,0:T(1,128)S(1)} %copy-done.4, bf16[128,24,128]{2,1,0:T(8,128)(2,1)S(1)} %all_to_all.11.g_ref, bf16[512,64]{1,0:T(8,128)(2,1)S(1)} %copy-done.3, bf16[64,1024]{1,0:T(8,128)(2,1)S(1)} %copy-done.2), custom_call_target="tpu_custom_call" | custom-call | flops 900000000 | bytes 12000000 | tf_op jit(solution)/shard_map/pair_lags/pallas_call | solution.py:364
Async XLA Ops:
  0.0 30.1 %copy-start = (bf16[640,1536]{1,0:T(8,128)(2,1)S(1)}, bf16[640,1536]{1,0:T(8,128)(2,1)}, u32[]{:S(2)}) copy-start(bf16[640,1536]{1,0:T(8,128)(2,1)} %constant.15.clone.table_ref) | copy-start | bytes 5898244
  0.0 30.1 %copy-start.5 = (f32[1,512]{1,0:T(1,128)S(1)}, f32[1,512]{1,0:T(1,128)}, u32[]{:S(2)}) copy-start(f32[1,512]{1,0:T(1,128)} %constant.14.clone.taper_ref) | copy-start | bytes 6148
  0.0 30.1 %copy-start.1 = (bf16[256,320]{1,0:T(8,128)(2,1)S(1)}, bf16[256,320]{1,0:T(8,128)(2,1)}, u32[]{:S(2)}) copy-start(bf16[256,320]{1,0:T(8,128)(2,1)} %constant.13.clone.ones_ref) | copy-start | bytes 491524
  0.0 54.4 %copy-start.2 = (bf16[64,1024]{1,0:T(8,128)(2,1)S(1)}, bf16[64,1024]{1,0:T(8,128)(2,1)}, u32[]{:S(2)}) copy-start(bf16[64,1024]{1,0:T(8,128)(2,1)} %constant.17.clone.back_ref) | copy-start | bytes 393220
  0.0 54.4 %copy-start.3 = (bf16[512,64]{1,0:T(8,128)(2,1)S(1)}, bf16[512,64]{1,0:T(8,128)(2,1)}, u32[]{:S(2)}) copy-start(bf16[512,64]{1,0:T(8,128)(2,1)} %constant.16.clone.reduce_ref) | copy-start | bytes 196612
  0.0 54.4 %copy-start.4 = (s32[2,1,2]{2,1,0:T(1,128)S(1)}, s32[2,1,2]{2,1,0:T(1,128)}, u32[]{:S(2)}) copy-start(s32[2,1,2]{2,1,0:T(1,128)} %pairs_ref.1) | copy-start | bytes 52
